TPU v7x, 32 devices: a whole 2x2x4 slice. The times are simulated.
32 devices in a mesh: face: 4 (over y, x), col: 8 (over z, core).
Axes of the slice: x: 2, y: 2, z: 4, core: 2. Of those that a mesh axis runs over, the one named last changes fastest.
Arguments:
- dyn_state: float32 [16, 64, 16, 720], P('face', 'col'), may hold values from -6 to 6
- edge_links: int32 [16, 64, 4], P('face', 'col'), may hold values from 0 to 8191, as said below
- phys_slot: int32 [16, 64, 4], P('face', 'col'), may hold values from 0 to 4095, as said below
- crm_active: int32 [4096], P(('face', 'col')), may hold values 0 or 1
- crm_state: bfloat16 [10, 32, 64, 4096], P(None, None, None, ('face', 'col')), may hold values from -4 to 4
Outputs:
- dyn_new: float32 [16, 64, 16, 720], P('face', 'col')
- column_tend: float32 [16, 64, 4, 320], P('face', 'col')
- crm_new: bfloat16 [10, 32, 64, 4096], P(None, None, None, ('face', 'col'))
Inputs may be any that keep to these rules, and one draw needn't show every extreme that they name: `edge_links`: each entry is 8 n + 2 k' + r: element n (id row * 64 + column in a grid of 16 x 64 elements), its edge k' (0 to 3) and a reversal bit r. For edge 0 of element (row, column) n lies in row - 1, for edge 2 in row + 1, for edge 1 in column + 1, for edge 3 in column - 1, rows modulo 16 and columns modulo 64; the other coordinate differs by at most one. `phys_slot`: A permutation of the physics columns. The physics column p lives on device p // 128 of face+col; of the quadrants on one device of the element layout exactly 4 go to each device.
All inputs are finite; a program needn't handle non-finite values. No bound on the sum of `crm_active` on one device may be relied on, other than what follows from the above.
Results may differ from a plain program's by a relative error of at most 0.001.
Values sent between devices are 32-bit elements; how exact they have to be, the bound alone decides.
A program may use at most 192 MiB of HBM per device.

v0:
```python
import jax
import jax.numpy as jnp
import numpy as np
from jax import lax
from jax.sharding import PartitionSpec as P

NFLD = 10
LEV = 72
CLEV = 32
DSTEPS = 2
CSTEPS = 2


KAPPA = 0.1
ADVECT = 0.1
DIFF_X = 0.2
DIFF_Z = 0.1
RELAX = 0.2
CONVERT = 0.5


def extended_2(cells, sides, width):
    for axis, dim in sides:
        count = lax.axis_size(axis)
        head = lax.slice_in_dim(cells, 0, width, axis=dim)
        tail = lax.slice_in_dim(cells, cells.shape[dim] - width, cells.shape[dim], axis=dim)
        cells = jnp.concatenate(
            [
                lax.ppermute(tail, axis, [(i, (i + 1) % count) for i in range(count)]),
                cells,
                lax.ppermute(head, axis, [((i + 1) % count, i) for i in range(count)]),
            ],
            axis=dim,
        )
    return cells


def node_tables():
    laplace = np.zeros((16, 16), np.float32)
    for row_a in range(4):
        for row_b in range(4):
            here = row_a * 4 + row_b
            for step_a, step_b in ((1, 0), (-1, 0), (0, 1), (0, -1)):
                near_a, near_b = (row_a + step_a, row_b + step_b)
                if 0 <= near_a < 4 and 0 <= near_b < 4:
                    laplace[here, near_a * 4 + near_b] += 1.0
                    laplace[here, here] -= 1.0
    edge_nodes = np.array([[0, 1, 2, 3], [3, 7, 11, 15], [12, 13, 14, 15], [0, 4, 8, 12]])
    spread = np.zeros((16, 16), np.float32)
    for edge in range(4):
        for point in range(4):
            spread[edge_nodes[edge, point], edge * 4 + point] = 1.0
    denom = 1.0 + spread.sum(axis=1)
    quarter = np.zeros((4, 16), np.float32)
    for row_a in range(4):
        for row_b in range(4):
            quarter[row_a // 2 * 2 + row_b // 2, row_a * 4 + row_b] = 0.25
    return (laplace, spread, denom, quarter)


def matched_points(links):
    other_edge = links // 2 % 4
    reversal = links % 2
    points = jnp.arange(4, dtype=jnp.int32)
    along = jnp.where(reversal[..., None] == 1, 3 - points, points)
    base = jnp.where(other_edge == 1, 3, jnp.where(other_edge == 2, 12, 0))
    stride = jnp.where((other_edge == 1) | (other_edge == 3), 4, 1)
    return base[..., None] + stride[..., None] * along


def crm_run(state, forcing, active):
    start_mean = jnp.mean(state, axis=2)
    live = (active == 1)[None, None, None, :]
    for step in range(CSTEPS):
        east = jnp.roll(state, -1, axis=2)
        west = jnp.roll(state, 1, axis=2)
        upper = jnp.concatenate([state[:, 1:], state[:, -1:]], axis=1)
        lower = jnp.concatenate([state[:, :1], state[:, :-1]], axis=1)
        mean_x = jnp.mean(state, axis=2, keepdims=True)
        fresh = (
            state
            - ADVECT * state[0:1] * (east - west)
            + DIFF_X * (east + west - 2.0 * state)
            + DIFF_Z * (upper + lower - 2.0 * state)
            + RELAX * (forcing[:, :, None, :] - mean_x)
        )
        cond = CONVERT * jnp.maximum(fresh[3:4] - fresh[2:3], 0.0)
        fresh = jnp.concatenate(
            [fresh[:3], fresh[3:4] - cond, fresh[4:5] + cond, fresh[5:]], axis=0
        )
        state = jnp.where(live, fresh, state)
    tend = (jnp.mean(state, axis=2) - start_mean) / CSTEPS
    return (state, tend)


def per_device(dyn_state, edge_links, phys_slot, crm_active, crm_state):
    laplace, spread, denom, quarter = [jnp.asarray(table) for table in node_tables()]
    rows_dev, cols_dev, nodes, width = dyn_state.shape
    nface = lax.axis_size("face")
    ncol = lax.axis_size("col")
    ndev = nface * ncol
    total_rows = rows_dev * nface
    total_cols = cols_dev * ncol
    neighbour = edge_links // 8
    pick = matched_points(edge_links)
    near_row = neighbour // total_cols
    near_col = neighbour % total_cols
    local_row = lax.broadcasted_iota(jnp.int32, (rows_dev, cols_dev, 4), 0)
    local_col = lax.broadcasted_iota(jnp.int32, (rows_dev, cols_dev, 4), 1)
    drow = (near_row - (lax.axis_index("face") * rows_dev + local_row) + 1) % total_rows - 1
    dcol = (near_col - (lax.axis_index("col") * cols_dev + local_col) + 1) % total_cols - 1
    place = (local_row + drow + 1) * (cols_dev + 2) + (local_col + dcol + 1)
    index_flat = place[..., None] * 16 + pick
    index_flat = index_flat.reshape(-1)
    state = dyn_state
    for step in range(DSTEPS):
        state = state + KAPPA * jnp.einsum(
            "nm,rcmw->rcnw", laplace, state, precision=lax.Precision.HIGHEST
        )
        extended = extended_2(state, (("face", 0), ("col", 1)), 1)
        matched = jnp.take(extended.reshape(-1, width), index_flat, axis=0).reshape(
            rows_dev, cols_dev, 16, width
        )
        summed = jnp.einsum("nm,rcmw->rcnw", spread, matched, precision=lax.Precision.HIGHEST)
        state = (state + summed) / denom[None, None, :, None]
    columns = jnp.einsum("qn,rcnw->rcqw", quarter, state, precision=lax.Precision.HIGHEST).reshape(
        -1, width
    )
    per_dev = columns.shape[0]
    count = per_dev // ndev
    keys_local = phys_slot.reshape(-1)
    order = jnp.argsort(keys_local, stable=True)
    outgoing = columns[order]
    out_keys = keys_local[order]
    arrived, arrived_keys = (
        lax.all_to_all(
            outgoing.reshape(ndev, count, width),
            ("face", "col"),
            split_axis=0,
            concat_axis=0,
            tiled=True,
        ),
        lax.all_to_all(
            out_keys.reshape(ndev, count), ("face", "col"), split_axis=0, concat_axis=0, tiled=True
        ),
    )
    slots = arrived_keys.reshape(-1) % per_dev
    physics = jnp.zeros((per_dev, width), jnp.float32).at[slots].set(arrived.reshape(-1, width))
    forcing = physics.reshape(per_dev, NFLD, LEV)[:, :, :CLEV].transpose(1, 2, 0)
    final, tend = crm_run(crm_state.astype(jnp.float32), forcing, crm_active)
    crm_new = final.astype(jnp.bfloat16)
    tend_rows = tend.reshape(NFLD * CLEV, per_dev).T[slots]
    returned = lax.all_to_all(
        tend_rows.reshape(ndev, count, NFLD * CLEV),
        ("face", "col"),
        split_axis=0,
        concat_axis=0,
        tiled=True,
    )
    placed = (
        jnp.zeros((per_dev, NFLD * CLEV), jnp.float32)
        .at[order]
        .set(returned.reshape(per_dev, NFLD * CLEV))
    )
    column_tend = placed.reshape(rows_dev, cols_dev, 4, NFLD * CLEV)
    return (state, column_tend, crm_new)


def solution(mesh):
    return jax.shard_map(
        per_device,
        mesh=mesh,
        in_specs=(
            P("face", "col", None, None),
            P("face", "col", None),
            P("face", "col", None),
            P(("face", "col")),
            P(None, None, None, ("face", "col")),
        ),
        out_specs=(
            P("face", "col", None, None),
            P("face", "col", None, None),
            P(None, None, None, ("face", "col")),
        ),
        check_vma=False,
    )
```

profile of v0, /device:TPU:1, one launch (start us, length us, event | category | flops | bytes accessed | tf_op | source)
XLA Modules:
  0.0 216.2 jit_solution(11216164300678633471)
XLA Ops:
  0.6 3.4 %bitcast_add_fusion.3 = f32[4,8,16,720]{3,2,1,0:T(8,128)S(1)} fusion(f32[4,8,16,720]{3,2,1,0:T(8,128)} %param.11, f32[16,16,1,1]{1,0,3,2:T(8,128)} %constant.173), kind=kOutput, calls=%fused_computation.31 | convolution fusion | flops 71516160 | bytes 2950144 | tf_op jit(solution)/shard_map/nm,rcmw->rcnw/dot_general | solution.py:117
  4.1 2.1 collective-permute-start
  8.2 2.5 %sort.17 = (s32[128]{0:T(128)}, s32[128]{0:T(128)S(1)}) sort(s32[128]{0:T(128)S(1)} %reshape.157, s32[128]{0:T(128)S(1)} %iota.35), dimensions={0}, to_apply=%region_0.2 | sort | flops 896 | bytes 2048 | tf_op jit(solution)/shard_map/jit(argsort)/sort | solution.py:132
  12.7 6.1 %all-to-all-start = ((s32[32,1,4]{2,1,0:T(1,128)}), s32[32,1,4]{2,1,0:T(1,128)S(1)}, u32[]{:S(2)}, u32[]{:S(2)}) async-start(s32[32,1,4]{2,1,0:T(1,128)} %bitcast.15), calls=%async_computation | async-start | bytes 32768 | tf_op jit(solution)/shard_map/all_to_all | solution.py:143
  18.7 14.9 %fusion.50 = (f32[10,32,63,128]{3,2,1,0:T(8,128)}, f32[10,32,63,128]{3,2,1,0:T(8,128)}) fusion(bf16[10,32,64,128]{3,2,1,0:T(8,128)(2,1)} %param.15), kind=kLoop, calls=%fused_computation.135 | loop fusion | bytes 41287680 | tf_op jit(solution)/shard_map/jit(_roll_static)/slice | solution.py:75
  33.6 13.5 %fusion.53 = (f32[10,31,64,128]{3,2,1,0:T(8,128)}, f32[10,31,64,128]{3,2,1,0:T(8,128)}) fusion(bf16[10,32,64,128]{3,2,1,0:T(8,128)(2,1)} %param.15), kind=kLoop, calls=%fused_computation.138 | loop fusion | bytes 40632320 | tf_op jit(solution)/shard_map/slice | solution.py:78
  49.8 4.3 %collective-permute-done.2 = f32[6,1,16,720]{3,2,1,0:T(8,128)S(1)} collective-permute-done((f32[6,1,16,720]{3,2,1,0:T(8,128)S(1)}, f32[6,1,16,720]{3,2,1,0:T(8,128)S(1)}, u32[]{:S(2)}, u32[]{:S(2)}) %collective-permute-start.2) | collective-permute-done | bytes 276512 | tf_op jit(solution)/shard_map/ppermute | solution.py:29
  54.1 4.7 %collective-permute-done.3 = f32[6,1,16,720]{3,2,1,0:T(8,128)S(1)} collective-permute-done((f32[6,1,16,720]{3,2,1,0:T(8,128)S(1)}, f32[6,1,16,720]{3,2,1,0:T(8,128)S(1)}, u32[]{:S(2)}, u32[]{:S(2)}) %collective-permute-start.3) | collective-permute-done | bytes 276512 | tf_op jit(solution)/shard_map/ppermute | solution.py:31
  58.8 1.8 pad_maximum_fusion.4
  60.6 2.6 %gather_fusion.3 = f32[512,720]{1,0:T(8,128)} fusion(f32[960,720]{1,0:T(8,128)S(1)} %bitcast.61, s32[1024]{0:T(1024)S(1)} %pad_clamp_fusion.2), kind=kCustom, calls=%fused_computation.clone | custom fusion | bytes 2951168 | tf_op jit(solution)/shard_map/jit(_take)/gather | solution.py:121
  63.2 1.7 broadcast_select_fusion.1
  66.5 3.8 %bitcast_add_fusion.1 = f32[4,8,16,720]{3,2,1,0:T(8,128)S(1)} fusion(f32[16,16,1,1]{1,0,3,2:T(8,128)S(1)} %copy-done.14, f32[4,8,16,720]{3,2,1,0:T(8,128)} %copy-done.3, f32[4,8,720,16]{2,3,1,0:T(8,128)S(1)} %fusion.56, f32[16]{0:T(128)S(1)} %copy-done.17), kind=kOutput, calls=%fused_computation.28 | convolution fusion | flops 72990720 | bytes 4424768 | tf_op jit(solution)/shard_map/nm,rcmw->rcnw/dot_general | solution.py:117
  72.8 1.9 fusion.52
  76.3 5.8 %collective-permute-done.4 = f32[1,8,16,720]{3,2,1,0:T(8,128)S(1)} collective-permute-done((f32[1,8,16,720]{3,2,1,0:T(8,128)S(1)}, f32[1,8,16,720]{3,2,1,0:T(8,128)S(1)}, u32[]{:S(2)}, u32[]{:S(2)}) %collective-permute-start.4) | collective-permute-done | bytes 368672 | tf_op jit(solution)/shard_map/ppermute | solution.py:29
  82.1 8.0 %collective-permute-done.5 = f32[1,8,16,720]{3,2,1,0:T(8,128)S(1)} collective-permute-done((f32[1,8,16,720]{3,2,1,0:T(8,128)S(1)}, f32[1,8,16,720]{3,2,1,0:T(8,128)S(1)}, u32[]{:S(2)}, u32[]{:S(2)}) %collective-permute-start.5) | collective-permute-done | bytes 368672 | tf_op jit(solution)/shard_map/ppermute | solution.py:31
  92.9 3.6 %collective-permute-done.6 = f32[6,1,16,720]{3,2,1,0:T(8,128)S(1)} collective-permute-done((f32[6,1,16,720]{3,2,1,0:T(8,128)S(1)}, f32[6,1,16,720]{3,2,1,0:T(8,128)S(1)}, u32[]{:S(2)}, u32[]{:S(2)}) %collective-permute-start.6) | collective-permute-done | bytes 276512 | tf_op jit(solution)/shard_map/ppermute | solution.py:29
  96.4 4.4 %collective-permute-done.7 = f32[6,1,16,720]{3,2,1,0:T(8,128)S(1)} collective-permute-done((f32[6,1,16,720]{3,2,1,0:T(8,128)S(1)}, f32[6,1,16,720]{3,2,1,0:T(8,128)S(1)}, u32[]{:S(2)}, u32[]{:S(2)}) %collective-permute-start.7) | collective-permute-done | bytes 276512 | tf_op jit(solution)/shard_map/ppermute | solution.py:31
  101.1 2.6 %gather_fusion.4 = f32[512,720]{1,0:T(8,128)} fusion(f32[960,720]{1,0:T(8,128)S(1)} %bitcast.60, s32[1024]{0:T(1024)S(1)} %pad_clamp_fusion.2), kind=kCustom, calls=%fused_computation.1.clone | custom fusion | bytes 2951168 | tf_op jit(solution)/shard_map/jit(_take)/gather | solution.py:121
  105.3 3.0 %fusion.8 = f32[4,8,16,720]{3,2,1,0:T(8,128)S(1)} fusion(f32[4,8,16,720]{3,2,1,0:T(8,128)} %copy-done.4, f32[4,8,16,720]{3,2,1,0:T(8,128)S(1)} %bitcast.63, f32[16,16,1,1]{1,0,3,2:T(8,128)S(1)} %copy-done.13, f32[16]{0:T(128)S(1)} %copy-done.17), kind=kOutput, calls=%fused_computation.27 | convolution fusion | flops 71516160 | bytes 4424768 | tf_op jit(solution)/shard_map/nm,rcmw->rcnw/dot_general | solution.py:124
  112.3 2.9 %all-to-all-start.1 = ((f32[32,4,720]{2,1,0:T(4,128)}), f32[32,4,720]{2,1,0:T(4,128)S(1)}, u32[]{:S(2)}, u32[]{:S(2)}) async-start(f32[32,4,720]{2,1,0:T(4,128)} %reshape.160), calls=%async_computation.1 | async-start | bytes 786432 | tf_op jit(solution)/shard_map/all_to_all | solution.py:136
  115.2 4.5 %convert_reduce_fusion = f32[10,32,128]{2,1,0:T(8,128)S(1)} fusion(bf16[10,32,64,128]{3,2,1,0:T(8,128)(2,1)} %param.15), kind=kLoop, calls=%fused_computation.23 | loop fusion | flops 5201920 | bytes 5406720 | tf_op jit(solution)/shard_map/reduce_sum | solution.py:79
  121.0 7.6 %all-to-all-done.1 = f32[32,4,720]{2,1,0:T(4,128)S(1)} async-done(((f32[32,4,720]{2,1,0:T(4,128)}), f32[32,4,720]{2,1,0:T(4,128)S(1)}, u32[]{:S(2)}, u32[]{:S(2)}) %all-to-all-start.1) | async-done | bytes 368672 | tf_op jit(solution)/shard_map/all_to_all | solution.py:136
  131.0 16.4 %fusion.3 = f32[10,32,64,128]{3,2,1,0:T(8,128)S(1)} fusion(f32[10,1,64,128]{3,2,1,0:T(8,128)S(1)} %copy-done.12, f32[10,31,64,128]{3,2,1,0:T(8,128)} %get-tuple-element.29, f32[10,31,64,128]{3,2,1,0:T(8,128)} %get-tuple-element.28, f32[10,1,64,128]{3,2,1,0:T(8,128)S(1)} %copy-done.11, f32[10,32,63,128]{3,2,1,0:T(8,128)} %get-tuple-element.23, ...), kind=kLoop, calls=%fused_computation.13 | loop fusion | flops 47185920 | bytes 58884096 | tf_op jit(solution)/shard_map/add | solution.py:81
  150.3 4.8 %fusion.45 = (f32[10,32,128]{2,1,0:T(8,128)S(1)}, f32[10,32,64,128]{3,2,1,0:T(8,128)S(1)}) fusion(bf16[10,32,64,128]{3,2,1,0:T(8,128)(2,1)S(1)} %bitcast.59, f32[5,32,64,128]{3,2,1,0:T(8,128)S(1)} %slice.182, f32[1,32,64,128]{3,2,1,0:T(8,128)} %get-tuple-element.21, f32[1,32,64,128]{3,2,1,0:T(8,128)S(1)} %get-tuple-element.20, ...), kind=kLoop, calls=%fused_computation.130 | loop fusion | flops 15687680 | bytes 26378368 | tf_op jit(solution)/shard_map/reduce_sum | solution.py:79
  155.1 8.7 %fusion.46 = (f32[10,32,63,128]{3,2,1,0:T(8,128)}, f32[10,32,63,128]{3,2,1,0:T(8,128)}) fusion(f32[10,32,64,128]{3,2,1,0:T(8,128)S(1)} %get-tuple-element.7), kind=kLoop, calls=%fused_computation.131 | loop fusion | bytes 41287680 | tf_op jit(solution)/shard_map/jit(_roll_static)/slice | solution.py:75
  163.8 8.1 %fusion.49 = (f32[10,31,64,128]{3,2,1,0:T(8,128)}, f32[10,31,64,128]{3,2,1,0:T(8,128)}) fusion(f32[10,32,64,128]{3,2,1,0:T(8,128)S(1)} %get-tuple-element.7), kind=kLoop, calls=%fused_computation.134 | loop fusion | bytes 40632320 | tf_op jit(solution)/shard_map/slice | solution.py:78
  173.4 18.4 %fusion.7 = f32[10,32,64,128]{3,2,1,0:T(8,128)} fusion(f32[10,1,64,128]{3,2,1,0:T(8,128)S(1)} %get-tuple-element.17, f32[10,31,64,128]{3,2,1,0:T(8,128)} %get-tuple-element.19, f32[10,31,64,128]{3,2,1,0:T(8,128)} %get-tuple-element.18, f32[10,1,64,128]{3,2,1,0:T(8,128)S(1)} %get-tuple-element.16, f32[10,32,64,128]{3,2,1,0:T(8,128)S(1)} %get-tuple-element.7, ...), kind=kLoop, calls=%fused_computation.21 | loop fusion | flops 44564480 | bytes 64126976 | tf_op jit(solution)/shard_map/add | solution.py:81
  191.8 3.1 %slice.196 = f32[5,32,64,128]{3,2,1,0:T(8,128)S(1)} slice(f32[10,32,64,128]{3,2,1,0:T(8,128)} %fusion.7), slice={[5:10], [0:32], [0:64], [0:128]} | slice | bytes 10485760 | tf_op jit(solution)/shard_map/slice | solution.py:89
  194.9 2.4 %copy-done.2 = f32[10,32,64,128]{3,2,1,0:T(8,128)S(1)} copy-done((f32[10,32,64,128]{3,2,1,0:T(8,128)S(1)}, f32[10,32,64,128]{3,2,1,0:T(8,128)}, u32[]{:S(2)}) %copy-start.2) | copy-done | bytes 10485784
  198.0 2.2 %fusion.19 = f32[10,32,128]{2,1,0:T(8,128)S(1)} fusion(f32[10,32,64,128]{3,2,1,0:T(8,128)S(1)} %get-tuple-element.7, f32[5,32,64,128]{3,2,1,0:T(8,128)S(1)} %slice.196, f32[1,32,64,128]{3,2,1,0:T(8,128)S(1)} %get-tuple-element.11, f32[1,32,64,128]{3,2,1,0:T(8,128)S(1)} %get-tuple-element.10, f32[3,32,64,128]{3,2,1,0:T(8,128)S(1)} %slice.192, ...), kind=kLoop, calls=%fused_computation.57 | loop fusion | flops 13066240 | bytes 21135488 | tf_op jit(solution)/shard_map/reduce_sum | solution.py:92
  202.0 2.6 %all-to-all-start.2 = ((f32[32,4,320]{2,1,0:T(4,128)}), f32[32,4,320]{2,1,0:T(4,128)S(1)}, u32[]{:S(2)}, u32[]{:S(2)}) async-start(f32[32,4,320]{2,1,0:T(4,128)} %reshape.163), calls=%async_computation.2 | async-start | bytes 393216 | tf_op jit(solution)/shard_map/all_to_all | solution.py:153
  204.6 9.7 %fusion.18 = bf16[10,32,64,128]{3,2,1,0:T(8,128)(2,1)} fusion(f32[10,32,64,128]{3,2,1,0:T(8,128)} %copy-done, f32[5,32,64,128]{3,2,1,0:T(8,128)} %copy-done.1, f32[1,32,64,128]{3,2,1,0:T(8,128)} %copy-done.6, f32[1,32,64,128]{3,2,1,0:T(8,128)} %copy-done.5, f32[3,32,64,128]{3,2,1,0:T(8,128)S(1)} %slice.192, pred[128]{0:T(512)(128)(4,1)S(1)} %broadcast_compare_fusion.2), kind=kLoop, calls=%fused_computation.56 | loop fusion | flops 23592960 | bytes 26214528 | tf_op jit(solution)/shard_map/convert_element_type | solution.py:151
  (120 shorter events, 33.0 us)
Async XLA Ops:
  4.1 43.9 %copy-start.3 = (f32[4,8,16,720]{3,2,1,0:T(8,128)}, f32[4,8,16,720]{3,2,1,0:T(8,128)S(1)}, u32[]{:S(2)}) copy-start(f32[4,8,16,720]{3,2,1,0:T(8,128)S(1)} %bitcast_add_fusion.3) | copy-start | bytes 4423684
  4.1 43.8 %collective-permute-start = (f32[1,8,16,720]{3,2,1,0:T(8,128)S(1)}, f32[1,8,16,720]{3,2,1,0:T(8,128)S(1)}, u32[]{:S(2)}, u32[]{:S(2)}) collective-permute-start(f32[1,8,16,720]{3,2,1,0:T(8,128)S(1)} %get-tuple-element.36), channel_id=1, source_target_pairs={{0,8},{8,16},{16,24},{24,0},{1,9},{9,17},{17,25},{25,1},{2,10},{10... | collective-permute-start | bytes 1105928 | tf_op jit(solution)/shard_map/ppermute | solution.py:29
  6.2 41.8 %collective-permute-start.1 = (f32[1,8,16,720]{3,2,1,0:T(8,128)S(1)}, f32[1,8,16,720]{3,2,1,0:T(8,128)S(1)}, u32[]{:S(2)}, u32[]{:S(2)}) collective-permute-start(f32[1,8,16,720]{3,2,1,0:T(8,128)S(1)} %get-tuple-element.37), channel_id=1, source_target_pairs={{8,0},{16,8},{24,16},{0,24},{9,1},{17,9},{25,17},{1,25},{10,2},{18... | collective-permute-start | bytes 1105928 | tf_op jit(solution)/shard_map/ppermute | solution.py:31
  12.7 99.7 %all-to-all-start = ((s32[32,1,4]{2,1,0:T(1,128)}), s32[32,1,4]{2,1,0:T(1,128)S(1)}, u32[]{:S(2)}, u32[]{:S(2)}) async-start(s32[32,1,4]{2,1,0:T(1,128)} %bitcast.15), calls=%async_computation | async-start | bytes 32768 | tf_op jit(solution)/shard_map/all_to_all | solution.py:143
  33.6 13.5 %copy-start.15 = (s32[4,8,4]{1,2,0:T(4,128)S(1)}, s32[4,8,4]{1,2,0:T(4,128)}, u32[]{:S(2)}) copy-start(s32[4,8,4]{1,2,0:T(4,128)} %param.12) | copy-start | bytes 1540
  48.0 6.1 %copy-start.9 = (f32[1,8,16,720]{3,2,1,0:T(8,128)}, f32[1,8,16,720]{3,2,1,0:T(8,128)S(1)}, u32[]{:S(2)}) copy-start(f32[1,8,16,720]{3,2,1,0:T(8,128)S(1)} %collective-permute-done.1) | copy-start | bytes 1105924
  48.1 6.0 %collective-permute-start.2 = (f32[6,1,16,720]{3,2,1,0:T(8,128)S(1)}, f32[6,1,16,720]{3,2,1,0:T(8,128)S(1)}, u32[]{:S(2)}, u32[]{:S(2)}) collective-permute-start(f32[6,1,16,720]{3,2,1,0:T(8,128)S(1)} %get-tuple-element.32), channel_id=1, source_target_pairs={{0,1},{1,2},{2,3},{3,4},{4,5},{5,6},{6,7},{7,0},{8,9},{9,10},{10,1... | collective-permute-start | bytes 829448 | tf_op jit(solution)/shard_map/ppermute | solution.py:29
  49.8 9.0 %collective-permute-start.3 = (f32[6,1,16,720]{3,2,1,0:T(8,128)S(1)}, f32[6,1,16,720]{3,2,1,0:T(8,128)S(1)}, u32[]{:S(2)}, u32[]{:S(2)}) collective-permute-start(f32[6,1,16,720]{3,2,1,0:T(8,128)S(1)} %get-tuple-element.33), channel_id=1, source_target_pairs={{1,0},{2,1},{3,2},{4,3},{5,4},{6,5},{7,6},{0,7},{9,8},{10,9},{11,1... | collective-permute-start | bytes 829448 | tf_op jit(solution)/shard_map/ppermute | solution.py:31
  49.8 15.2 %copy-start.13 = (f32[16,16,1,1]{1,0,3,2:T(8,128)S(1)}, f32[16,16,1,1]{1,0,3,2:T(8,128)}, u32[]{:S(2)}) copy-start(f32[16,16,1,1]{1,0,3,2:T(8,128)} %constant.174) | copy-start | bytes 3076
  60.6 5.8 %copy-start.14 = (f32[16,16,1,1]{1,0,3,2:T(8,128)S(1)}, f32[16,16,1,1]{1,0,3,2:T(8,128)}, u32[]{:S(2)}) copy-start(f32[16,16,1,1]{1,0,3,2:T(8,128)} %constant.173) | copy-start | bytes 3076
  60.6 5.8 %copy-start.17 = (f32[16]{0:T(128)S(1)}, f32[16]{0:T(128)}, u32[]{:S(2)}) copy-start(f32[16]{0:T(128)} %constant.171) | copy-start | bytes 196
  63.2 11.5 %slice-start = ((s8[5242880]{0:T(1024)(128)(4,1)}), s8[4194304]{0:T(1024)(128)(4,1)S(1)}, s32[]{:S(2)}) async-start(s8[5242880]{0:T(1024)(128)(4,1)} %bitcast.56), calls=%async_computation.3 | async-start | bytes 8388608
  66.5 8.2 %slice-start.1 = ((s8[5242880]{0:T(1024)(128)(4,1)}), s8[1048576]{0:T(1024)(128)(4,1)S(1)}, s32[]{:S(2)}) async-start(s8[5242880]{0:T(1024)(128)(4,1)} %bitcast.56), calls=%async_computation.4 | async-start | bytes 2097152
  70.2 30.6 %copy-start.4 = (f32[4,8,16,720]{3,2,1,0:T(8,128)}, f32[4,8,16,720]{3,2,1,0:T(8,128)S(1)}, u32[]{:S(2)}) copy-start(f32[4,8,16,720]{3,2,1,0:T(8,128)S(1)} %bitcast_add_fusion.1) | copy-start | bytes 4423684
  70.3 11.8 %collective-permute-start.4 = (f32[1,8,16,720]{3,2,1,0:T(8,128)S(1)}, f32[1,8,16,720]{3,2,1,0:T(8,128)S(1)}, u32[]{:S(2)}, u32[]{:S(2)}) collective-permute-start(f32[1,8,16,720]{3,2,1,0:T(8,128)S(1)} %get-tuple-element.34), channel_id=1, source_target_pairs={{0,8},{8,16},{16,24},{24,0},{1,9},{9,17},{17,25},{25,1},{2,10},{10... | collective-permute-start | bytes 1105928 | tf_op jit(solution)/shard_map/ppermute | solution.py:29
  71.8 18.3 %collective-permute-start.5 = (f32[1,8,16,720]{3,2,1,0:T(8,128)S(1)}, f32[1,8,16,720]{3,2,1,0:T(8,128)S(1)}, u32[]{:S(2)}, u32[]{:S(2)}) collective-permute-start(f32[1,8,16,720]{3,2,1,0:T(8,128)S(1)} %get-tuple-element.35), channel_id=1, source_target_pairs={{8,0},{16,8},{24,16},{0,24},{9,1},{17,9},{25,17},{1,25},{10,2},{18... | collective-permute-start | bytes 1105928 | tf_op jit(solution)/shard_map/ppermute | solution.py:31
  90.1 6.3 %collective-permute-start.6 = (f32[6,1,16,720]{3,2,1,0:T(8,128)S(1)}, f32[6,1,16,720]{3,2,1,0:T(8,128)S(1)}, u32[]{:S(2)}, u32[]{:S(2)}) collective-permute-start(f32[6,1,16,720]{3,2,1,0:T(8,128)S(1)} %get-tuple-element.30), channel_id=1, source_target_pairs={{0,1},{1,2},{2,3},{3,4},{4,5},{5,6},{6,7},{7,0},{8,9},{9,10},{10,1... | collective-permute-start | bytes 829448 | tf_op jit(solution)/shard_map/ppermute | solution.py:29
  91.8 9.1 %collective-permute-start.7 = (f32[6,1,16,720]{3,2,1,0:T(8,128)S(1)}, f32[6,1,16,720]{3,2,1,0:T(8,128)S(1)}, u32[]{:S(2)}, u32[]{:S(2)}) collective-permute-start(f32[6,1,16,720]{3,2,1,0:T(8,128)S(1)} %get-tuple-element.31), channel_id=1, source_target_pairs={{1,0},{2,1},{3,2},{4,3},{5,4},{6,5},{7,6},{0,7},{9,8},{10,9},{11,1... | collective-permute-start | bytes 829448 | tf_op jit(solution)/shard_map/ppermute | solution.py:31
  101.1 8.4 %copy-start.16 = (f32[4,16,1,1]{1,0,3,2:T(4,128)S(1)}, f32[4,16,1,1]{1,0,3,2:T(4,128)}, u32[]{:S(2)}) copy-start(f32[4,16,1,1]{1,0,3,2:T(4,128)} %constant.175) | copy-start | bytes 772
  103.7 11.5 %copy-start.18 = (s32[128]{0:T(128)S(1)}, s32[128]{0:T(128)}, u32[]{:S(2)}) copy-start(s32[128]{0:T(128)} %param.14) | copy-start | bytes 1540
  105.3 25.6 %copy-start.8 = (f32[32,64,128]{2,1,0:T(8,128)S(1)}, f32[32,64,128]{2,1,0:T(8,128)}, u32[]{:S(2)}) copy-start(f32[32,64,128]{2,1,0:T(8,128)} %fusion.16) | copy-start | bytes 3145732
  105.3 25.6 %copy-start.11 = (f32[10,1,64,128]{3,2,1,0:T(8,128)S(1)}, f32[10,1,64,128]{3,2,1,0:T(8,128)}, u32[]{:S(2)}) copy-start(f32[10,1,64,128]{3,2,1,0:T(8,128)} %get-tuple-element.26) | copy-start | bytes 983044
  105.3 25.6 %copy-start.12 = (f32[10,1,64,128]{3,2,1,0:T(8,128)S(1)}, f32[10,1,64,128]{3,2,1,0:T(8,128)}, u32[]{:S(2)}) copy-start(f32[10,1,64,128]{3,2,1,0:T(8,128)} %get-tuple-element.27) | copy-start | bytes 983044
  112.3 16.3 %all-to-all-start.1 = ((f32[32,4,720]{2,1,0:T(4,128)}), f32[32,4,720]{2,1,0:T(4,128)S(1)}, u32[]{:S(2)}, u32[]{:S(2)}) async-start(f32[32,4,720]{2,1,0:T(4,128)} %reshape.160), calls=%async_computation.1 | async-start | bytes 786432 | tf_op jit(solution)/shard_map/all_to_all | solution.py:136
  147.4 2.6 %slice-start.2 = ((s8[5242880]{0:T(1024)(128)(4,1)}), s8[4194304]{0:T(1024)(128)(4,1)S(1)}, s32[]{:S(2)}) async-start(s8[5242880]{0:T(1024)(128)(4,1)} %bitcast.58), calls=%async_computation.5 | async-start | bytes 8388608
  147.8 2.5 %slice-start.3 = ((s8[5242880]{0:T(1024)(128)(4,1)}), s8[1048576]{0:T(1024)(128)(4,1)S(1)}, s32[]{:S(2)}) async-start(s8[5242880]{0:T(1024)(128)(4,1)} %bitcast.58), calls=%async_computation.6 | async-start | bytes 2097152
  155.1 42.9 %copy-start = (f32[10,32,64,128]{3,2,1,0:T(8,128)}, f32[10,32,64,128]{3,2,1,0:T(8,128)S(1)}, u32[]{:S(2)}) copy-start(f32[10,32,64,128]{3,2,1,0:T(8,128)S(1)} %get-tuple-element.7) | copy-start | bytes 31457284
  191.8 5.5 %copy-start.2 = (f32[10,32,64,128]{3,2,1,0:T(8,128)S(1)}, f32[10,32,64,128]{3,2,1,0:T(8,128)}, u32[]{:S(2)}) copy-start(f32[10,32,64,128]{3,2,1,0:T(8,128)} %fusion.7) | copy-start | bytes 31457284
  197.3 2.9 %copy-start.1 = (f32[5,32,64,128]{3,2,1,0:T(8,128)}, f32[5,32,64,128]{3,2,1,0:T(8,128)S(1)}, u32[]{:S(2)}) copy-start(f32[5,32,64,128]{3,2,1,0:T(8,128)S(1)} %slice.196) | copy-start | bytes 15728644
  198.0 2.3 %copy-start.5 = (f32[1,32,64,128]{3,2,1,0:T(8,128)}, f32[1,32,64,128]{3,2,1,0:T(8,128)S(1)}, u32[]{:S(2)}) copy-start(f32[1,32,64,128]{3,2,1,0:T(8,128)S(1)} %get-tuple-element.10) | copy-start | bytes 3145732
  198.0 2.3 %copy-start.6 = (f32[1,32,64,128]{3,2,1,0:T(8,128)}, f32[1,32,64,128]{3,2,1,0:T(8,128)S(1)}, u32[]{:S(2)}) copy-start(f32[1,32,64,128]{3,2,1,0:T(8,128)S(1)} %get-tuple-element.11) | copy-start | bytes 3145732
  202.0 12.3 %all-to-all-start.2 = ((f32[32,4,320]{2,1,0:T(4,128)}), f32[32,4,320]{2,1,0:T(4,128)S(1)}, u32[]{:S(2)}, u32[]{:S(2)}) async-start(f32[32,4,320]{2,1,0:T(4,128)} %reshape.163), calls=%async_computation.2 | async-start | bytes 393216 | tf_op jit(solution)/shard_map/all_to_all | solution.py:153
  (2 other events, 1.9 us)
where the time goes:
time: 217 us; the launch traced here: 216 us
  local copies, waits for them, and re-layouts  73.3 us (34%)
  other arithmetic  70.2 us (32%)
  waiting for transfers between devices  38.3 us (18%)
  starting transfers between devices  20.4 us (9%)
  matrix products  12.6 us (6%)
    add x2, other arithmetic, crm_run(): state - ADVECT * state[0:1] * (east - west)  34.8 us
    slice x4, local copies, waits for them, and re-layouts, crm_run(): east = jnp.roll(state, -1, axis=2)  24.2 us
    slice x4, local copies, waits for them, and re-layouts, crm_run(): lower = jnp.concatenate([state[:, :1], state[:, :-1]], axis=1)  23.6 us
    ppermute x4, waiting for transfers between devices, extended_2(): lax.ppermute(head, axis, [((i + 1) % count, i) for i in range(count)])  17.1 us
    ppermute x4, waiting for transfers between devices, extended_2(): lax.ppermute(tail, axis, [(i, (i + 1) % count) for i in range(count)])  13.6 us
    convert_element_type x1, other arithmetic, per_device(): crm_new = final.astype(jnp.bfloat16)  9.73 us
    reduce_sum x2, other arithmetic, crm_run(): mean_x = jnp.mean(state, axis=2, keepdims=True)  9.23 us
    all_to_all x1, waiting for transfers between devices, per_device(): lax.all_to_all(outgoing.reshape(ndev, count, width), ('face', 'col'), spl...  7.59 us
  transfers between devices with their start and end apart: 11, of which 7 were waited for; matrix products, arithmetic and copies ran while one was open for 35% of the time, Pallas kernels for 0%

commit v1 on v0

--- a/solution.py
+++ b/solution.py
@@ -2,6 +2,8 @@
 import jax.numpy as jnp
 import numpy as np
 from jax import lax
+from jax.experimental import pallas as pl
+from jax.experimental.pallas import tpu as pltpu
 from jax.sharding import PartitionSpec as P
 
 NFLD = 10
@@ -68,32 +70,111 @@
     return base[..., None] + stride[..., None] * along
 
 
+def crm_kernel(force_ref, active_ref, state_hbm, out_hbm, tend_ref, held, first, final, begin, in_sem, out_sem):
+    nfld, clev, cx, cols = held.shape
+    part = clev // 4
+
+    def fetch(i):
+        return pltpu.make_async_copy(
+            state_hbm.at[:, pl.ds(i * part, part)], held.at[:, pl.ds(i * part, part)], in_sem.at[i]
+        )
+
+    def emit(i):
+        return pltpu.make_async_copy(
+            final.at[:, pl.ds(i * part, part)], out_hbm.at[:, pl.ds(i * part, part)], out_sem.at[i]
+        )
+
+    for i in range(4):
+        fetch(i).start()
+    live = jnp.broadcast_to(active_ref[...] == 1, (cx, cols))
+
+    def advance(src, z, store):
+        above = jnp.minimum(z + 1, clev - 1)
+        below = jnp.maximum(z - 1, 0)
+        wind = ADVECT * src[0, z].astype(jnp.float32)
+        from_east = DIFF_X - wind
+        from_west = DIFF_X + wind
+
+        def one(f):
+            q = src[f, z].astype(jnp.float32)
+            mean = jnp.sum(q, axis=0, keepdims=True) * (1.0 / cx)
+            push = RELAX * (force_ref[f, pl.ds(z, 1), :] - mean)
+            near = src[f, above].astype(jnp.float32) + src[f, below].astype(jnp.float32)
+            fresh = (
+                (1.0 - 2.0 * DIFF_X - 2.0 * DIFF_Z) * q
+                + from_east * pltpu.roll(q, cx - 1, 0)
+                + from_west * pltpu.roll(q, 1, 0)
+                + DIFF_Z * near
+                + push
+            )
+            return q, fresh, mean
+
+        for f in range(nfld):
+            q, fresh, mean = one(f)
+            if f == 2:
+                second = fresh
+            if f == 3:
+                cond = CONVERT * jnp.maximum(fresh - second, 0.0)
+                fresh = fresh - cond
+            if f == 4:
+                fresh = fresh + cond
+            store(f, z, jnp.where(live, fresh, q), mean)
+
+    def store_first(f, z, value, mean):
+        first[f, z] = value
+        begin[f, pl.ds(z, 1), :] = mean
+
+    def store_final(f, z, value, mean):
+        final[f, z] = value.astype(final.dtype)
+        end = jnp.sum(value, axis=0, keepdims=True) * (1.0 / cx)
+        tend_ref[f, pl.ds(z, 1), :] = (end - begin[f, pl.ds(z, 1), :]) * (1.0 / CSTEPS)
+
+    fetch(0).wait()
+    fetch(1).wait()
+    advance(held, 0, store_first)
+    for i in range(4):
+        if 1 <= i < 3:
+            fetch(i + 1).wait()
+
+        @pl.loop(max(1, i * part), (i + 1) * part)
+        def _(z):
+            advance(held, z, store_first)
+            advance(first, z - 1, store_final)
+
+        if i >= 1:
+            emit(i - 1).start()
+    advance(first, clev - 1, store_final)
+    emit(3).start()
+    for i in range(4):
+        emit(i).wait()
+
+
 def crm_run(state, forcing, active):
-    start_mean = jnp.mean(state, axis=2)
-    live = (active == 1)[None, None, None, :]
-    for step in range(CSTEPS):
-        east = jnp.roll(state, -1, axis=2)
-        west = jnp.roll(state, 1, axis=2)
-        upper = jnp.concatenate([state[:, 1:], state[:, -1:]], axis=1)
-        lower = jnp.concatenate([state[:, :1], state[:, :-1]], axis=1)
-        mean_x = jnp.mean(state, axis=2, keepdims=True)
-        fresh = (
-            state
-            - ADVECT * state[0:1] * (east - west)
-            + DIFF_X * (east + west - 2.0 * state)
-            + DIFF_Z * (upper + lower - 2.0 * state)
-            + RELAX * (forcing[:, :, None, :] - mean_x)
-        )
-        cond = CONVERT * jnp.maximum(fresh[3:4] - fresh[2:3], 0.0)
-        fresh = jnp.concatenate(
-            [fresh[:3], fresh[3:4] - cond, fresh[4:5] + cond, fresh[5:]], axis=0
-        )
-        state = jnp.where(live, fresh, state)
-    tend = (jnp.mean(state, axis=2) - start_mean) / CSTEPS
-    return (state, tend)
+    nfld, clev, cx, cols = state.shape
+    vmem = pl.BlockSpec(memory_space=pltpu.VMEM)
+    hbm = pl.BlockSpec(memory_space=pl.ANY)
+    return pl.pallas_call(
+        crm_kernel,
+        out_shape=(
+            jax.ShapeDtypeStruct(state.shape, state.dtype),
+            jax.ShapeDtypeStruct((nfld, clev, cols), jnp.float32),
+        ),
+        in_specs=[vmem, vmem, hbm],
+        out_specs=(hbm, vmem),
+        scratch_shapes=[
+            pltpu.VMEM(state.shape, state.dtype),
+            pltpu.VMEM(state.shape, jnp.float32),
+            pltpu.VMEM(state.shape, state.dtype),
+            pltpu.VMEM((nfld, clev, cols), jnp.float32),
+            pltpu.SemaphoreType.DMA((4,)),
+            pltpu.SemaphoreType.DMA((4,)),
+        ],
+        compiler_params=pltpu.CompilerParams(vmem_limit_bytes=36 * 2**20),
+    )(forcing, active.reshape(1, cols), state)
 
 
 def per_device(dyn_state, edge_links, phys_slot, crm_active, crm_state):
+    exact = lax.Precision.HIGHEST
     laplace, spread, denom, quarter = [jnp.asarray(table) for table in node_tables()]
     rows_dev, cols_dev, nodes, width = dyn_state.shape
     nface = lax.axis_size("face")
@@ -123,46 +204,42 @@
         )
         summed = jnp.einsum("nm,rcmw->rcnw", spread, matched, precision=lax.Precision.HIGHEST)
         state = (state + summed) / denom[None, None, :, None]
-    columns = jnp.einsum("qn,rcnw->rcqw", quarter, state, precision=lax.Precision.HIGHEST).reshape(
-        -1, width
-    )
+    columns = jnp.einsum("qn,rcnw->rcqw", quarter, state, precision=exact).reshape(-1, width)
     per_dev = columns.shape[0]
     count = per_dev // ndev
+    depth = NFLD * CLEV
+    wanted = (np.arange(NFLD)[:, None] * LEV + np.arange(CLEV)).reshape(-1)
+    keep = jnp.asarray(np.arange(width)[:, None] == wanted[None, :], jnp.float32)
     keys_local = phys_slot.reshape(-1)
-    order = jnp.argsort(keys_local, stable=True)
-    outgoing = columns[order]
-    out_keys = keys_local[order]
-    arrived, arrived_keys = (
-        lax.all_to_all(
-            outgoing.reshape(ndev, count, width),
-            ("face", "col"),
-            split_axis=0,
-            concat_axis=0,
-            tiled=True,
-        ),
-        lax.all_to_all(
-            out_keys.reshape(ndev, count), ("face", "col"), split_axis=0, concat_axis=0, tiled=True
-        ),
+    rank = jnp.sum((keys_local[None, :] < keys_local[:, None]).astype(jnp.int32), axis=1)
+    sorting = rank[None, :] == jnp.arange(per_dev, dtype=jnp.int32)[:, None]
+    out_keys = jnp.sum(jnp.where(sorting, keys_local[None, :], 0), axis=1)
+    arrived_keys = lax.all_to_all(
+        out_keys.reshape(ndev, count), ("face", "col"), split_axis=0, concat_axis=0, tiled=True
     )
     slots = arrived_keys.reshape(-1) % per_dev
-    physics = jnp.zeros((per_dev, width), jnp.float32).at[slots].set(arrived.reshape(-1, width))
-    forcing = physics.reshape(per_dev, NFLD, LEV)[:, :, :CLEV].transpose(1, 2, 0)
-    final, tend = crm_run(crm_state.astype(jnp.float32), forcing, crm_active)
-    crm_new = final.astype(jnp.bfloat16)
-    tend_rows = tend.reshape(NFLD * CLEV, per_dev).T[slots]
-    returned = lax.all_to_all(
-        tend_rows.reshape(ndev, count, NFLD * CLEV),
+    landing = (slots[:, None] == jnp.arange(per_dev, dtype=jnp.int32)[None, :]).astype(jnp.float32)
+    sorting = sorting.astype(jnp.float32)
+    outgoing = jnp.dot(sorting, jnp.dot(columns, keep, precision=exact), precision=exact)
+    arrived = lax.all_to_all(
+        outgoing.reshape(ndev, count, depth),
         ("face", "col"),
         split_axis=0,
         concat_axis=0,
         tiled=True,
     )
-    placed = (
-        jnp.zeros((per_dev, NFLD * CLEV), jnp.float32)
-        .at[order]
-        .set(returned.reshape(per_dev, NFLD * CLEV))
-    )
-    column_tend = placed.reshape(rows_dev, cols_dev, 4, NFLD * CLEV)
+    forcing = jnp.einsum("sw,sc->wc", arrived.reshape(per_dev, depth), landing, precision=exact)
+    crm_new, tend = crm_run(crm_state, forcing.reshape(NFLD, CLEV, per_dev), crm_active)
+    tend_rows = jnp.einsum("sc,wc->sw", landing, tend.reshape(depth, per_dev), precision=exact)
+    returned = lax.all_to_all(
+        tend_rows.reshape(ndev, count, depth),
+        ("face", "col"),
+        split_axis=0,
+        concat_axis=0,
+        tiled=True,
+    )
+    placed = jnp.einsum("pi,pw->iw", sorting, returned.reshape(per_dev, depth), precision=exact)
+    column_tend = placed.reshape(rows_dev, cols_dev, 4, depth)
     return (state, column_tend, crm_new)
 
 

time: 217 us -> 139 us (0.64)
  other arithmetic: 70.2 us -> 8.49 us
  local copies, waits for them, and re-layouts: 73.3 us -> 13.8 us
  waiting for transfers between devices: 38.3 us -> 59 us
  Pallas kernels: 0 us -> 15.7 us
  blocking collectives: 0 us -> 12.1 us
  starting transfers between devices: 20.4 us -> 15.5 us
    slice x12 -> x0, local copies, waits for them, and re-layouts: 51.7 us -> none  [the longest x4 24.2 us: crm_run(): east = jnp.roll(state, -1, axis=2)]
    add x2 -> x0, other arithmetic: 34.8 us -> none  [crm_run(): state - ADVECT * state[0:1] * (east - west)]
    pallas_call x0 -> x1, Pallas kernels: none -> 15.7 us  [crm_run(): pl.pallas_call(crm_kernel, out_shape=(jax.ShapeDtypeStruct(state.shape, s...]
    all_to_all x0 -> x1, blocking collectives: none -> 12.1 us  [per_device(): lax.all_to_all(out_keys.reshape(ndev, count), ('face', 'col'), split_axis...]
    reduce_sum x3 -> x2, other arithmetic: 11.4 us -> 0.29 us  [the longest x1 0.18 us: per_device(): jnp.sum((keys_local[None, :] < keys_local[:, None]).astype(jnp.int32), ax...]
    convert_element_type x2 -> x0, other arithmetic: 11.1 us -> none  [the longest x1 9.73 us: per_device(): crm_new = final.astype(jnp.bfloat16)]
    all_to_all x3 -> x2, waiting for transfers between devices: 7.59 us -> 18.1 us  [the longest x1 9.33 us: per_device(): lax.all_to_all(outgoing.reshape(ndev, count, depth), ('face', 'col'), spl...]
    ppermute x4, waiting for transfers between devices: 13.6 us -> 21.4 us  [extended_2(): lax.ppermute(tail, axis, [(i, (i + 1) % count) for i in range(count)])]
  transfers between devices with their start and end apart: 11 -> 10, of which waited for: 7 -> 8; matrix products, arithmetic and copies ran while one was open for 35% -> 2% of each run, Pallas kernels for 0% -> 0%
where the time goes in v1:
time: 139 us
  waiting for transfers between devices  59 us (42%)
  Pallas kernels  15.7 us (11%)
  starting transfers between devices  15.5 us (11%)
  local copies, waits for them, and re-layouts  13.8 us (10%)
  matrix products  13 us (9%)
  blocking collectives  12.1 us (9%)
  other arithmetic  8.49 us (6%)
    ppermute x4, waiting for transfers between devices, extended_2(): lax.ppermute(tail, axis, [(i, (i + 1) % count) for i in range(count)])  21.4 us
    ppermute x4, waiting for transfers between devices, extended_2(): lax.ppermute(head, axis, [((i + 1) % count, i) for i in range(count)])  19.5 us
    pallas_call x1, Pallas kernels, crm_run(): pl.pallas_call(crm_kernel, out_shape=(jax.ShapeDtypeStruct(state.shape, s...  15.7 us
    all_to_all x1, blocking collectives, per_device(): lax.all_to_all(out_keys.reshape(ndev, count), ('face', 'col'), split_axis...  12.1 us
    all_to_all x1, waiting for transfers between devices, per_device(): lax.all_to_all(outgoing.reshape(ndev, count, depth), ('face', 'col'), spl...  9.33 us
    all_to_all x1, waiting for transfers between devices, per_device(): lax.all_to_all(tend_rows.reshape(ndev, count, depth), ('face', 'col'), sp...  8.74 us
    ppermute x4, starting transfers between devices, extended_2(): lax.ppermute(tail, axis, [(i, (i + 1) % count) for i in range(count)])  8.2 us
    dot_general x2, matrix products, per_device(): jnp.einsum('nm,rcmw->rcnw', laplace, state, precision=lax.Precision.HIGHEST)  5.19 us
  transfers between devices with their start and end apart: 10, of which 8 were waited for; matrix products, arithmetic and copies ran while one was open for 2% of the time, Pallas kernels for 0%

profile of v1, /device:TPU:1, one launch (start us, length us, event | category | flops | bytes accessed | tf_op | source)
XLA Modules:
  0.0 138.5 jit_solution(14665227932596118001)
XLA Ops:
  0.6 3.4 %bitcast_add_fusion.3 = f32[4,8,16,720]{3,2,1,0:T(8,128)S(1)} fusion(f32[4,8,16,720]{3,2,1,0:T(8,128)} %param.12, f32[16,16,1,1]{1,0,3,2:T(8,128)} %constant.150), kind=kOutput, calls=%fused_computation.9 | convolution fusion | flops 71516160 | bytes 2950144 | tf_op jit(solution)/shard_map/nm,rcmw->rcnw/dot_general | solution.py:198
  4.1 2.1 %collective-permute-start = (f32[1,8,16,720]{3,2,1,0:T(8,128)S(1)}, f32[1,8,16,720]{3,2,1,0:T(8,128)S(1)}, u32[]{:S(2)}, u32[]{:S(2)}) collective-permute-start(f32[1,8,16,720]{3,2,1,0:T(8,128)S(1)} %get-tuple-element.28), channel_id=1, source_target_pairs={{0,8},{8,16},{16,24},{24,0},{1,9},{9,17},{17,25},{25,1},{2,10},{10... | collective-permute-start | bytes 1105928 | tf_op jit(solution)/shard_map/ppermute | solution.py:31
  6.2 1.0 collective-permute-start.1
  8.1 7.9 %collective-permute-done = f32[1,8,16,720]{3,2,1,0:T(8,128)S(1)} collective-permute-done((f32[1,8,16,720]{3,2,1,0:T(8,128)S(1)}, f32[1,8,16,720]{3,2,1,0:T(8,128)S(1)}, u32[]{:S(2)}, u32[]{:S(2)}) %collective-permute-start) | collective-permute-done | bytes 368672 | tf_op jit(solution)/shard_map/ppermute | solution.py:31
  16.0 8.4 %collective-permute-done.1 = f32[1,8,16,720]{3,2,1,0:T(8,128)S(1)} collective-permute-done((f32[1,8,16,720]{3,2,1,0:T(8,128)S(1)}, f32[1,8,16,720]{3,2,1,0:T(8,128)S(1)}, u32[]{:S(2)}, u32[]{:S(2)}) %collective-permute-start.1) | collective-permute-done | bytes 368672 | tf_op jit(solution)/shard_map/ppermute | solution.py:33
  24.4 2.8 %collective-permute-start.2 = (f32[6,1,16,720]{3,2,1,0:T(8,128)S(1)}, f32[6,1,16,720]{3,2,1,0:T(8,128)S(1)}, u32[]{:S(2)}, u32[]{:S(2)}) collective-permute-start(f32[6,1,16,720]{3,2,1,0:T(8,128)S(1)} %get-tuple-element.24), channel_id=1, source_target_pairs={{0,1},{1,2},{2,3},{3,4},{4,5},{5,6},{6,7},{7,0},{8,9},{9,10},{10,1... | collective-permute-start | bytes 829448 | tf_op jit(solution)/shard_map/ppermute | solution.py:31
  27.2 4.2 %collective-permute-done.2 = f32[6,1,16,720]{3,2,1,0:T(8,128)S(1)} collective-permute-done((f32[6,1,16,720]{3,2,1,0:T(8,128)S(1)}, f32[6,1,16,720]{3,2,1,0:T(8,128)S(1)}, u32[]{:S(2)}, u32[]{:S(2)}) %collective-permute-start.2) | collective-permute-done | bytes 276512 | tf_op jit(solution)/shard_map/ppermute | solution.py:31
  31.4 5.0 %collective-permute-done.3 = f32[6,1,16,720]{3,2,1,0:T(8,128)S(1)} collective-permute-done((f32[6,1,16,720]{3,2,1,0:T(8,128)S(1)}, f32[6,1,16,720]{3,2,1,0:T(8,128)S(1)}, u32[]{:S(2)}, u32[]{:S(2)}) %collective-permute-start.3) | collective-permute-done | bytes 276512 | tf_op jit(solution)/shard_map/ppermute | solution.py:33
  36.4 1.8 %pad_maximum_fusion = f32[6,10,16,720]{3,2,1,0:T(8,128)S(1)} fusion(f32[6,1,16,720]{3,2,1,0:T(8,128)S(1)} %collective-permute-done.3, f32[1,8,16,720]{3,2,1,0:T(8,128)} %copy-done.7, f32[4,8,16,720]{3,2,1,0:T(8,128)} %copy-done.2, f32[1,8,16,720]{3,2,1,0:T(8,128)S(1)} %collective-permute-done, f32[6,1,16,720]{3,2,1,0:T(8,128)S(1)} %collective-permute-done.2), kind=kLoop, calls=%fused_computation.2 | loop fusion | flops 2764800 | bytes 5529600 | tf_op jit(solution)/shard_map/concatenate | solution.py:29
  38.2 2.6 %gather_fusion = f32[512,720]{1,0:T(8,128)} fusion(f32[960,720]{1,0:T(8,128)S(1)} %bitcast.70, s32[1024]{0:T(1024)S(1)} %pad_clamp_fusion), kind=kCustom, calls=%fused_computation.clone | custom fusion | bytes 2951168 | tf_op jit(solution)/shard_map/jit(_take)/gather | solution.py:202
  40.8 1.6 %broadcast_select_fusion.1 = f32[512,720]{1,0:T(8,128)S(1)} fusion(f32[512,720]{1,0:T(8,128)} %gather_fusion, pred[512]{0:T(512)(128)(4,1)S(1)} %compare_and_fusion), kind=kLoop, calls=%fused_computation.12 | loop fusion | flops 368640 | bytes 2949632 | tf_op jit(solution)/shard_map/jit(_take)/select_n | solution.py:202
  42.5 1.5 %fusion.41 = f32[4,8,720,16]{2,3,1,0:T(8,128)S(1)} fusion(f32[4,8,16,720]{3,2,1,0:T(8,128)S(1)} %bitcast.72, f32[16,16,1,1]{1,0,3,2:T(8,128)S(1)} %copy-done.11), kind=kOutput, calls=%fused_computation.102 | convolution fusion | flops 70778880 | bytes 2950144 | tf_op jit(solution)/shard_map/nm,rcmw->rcnw/dot_general | solution.py:205
  44.0 1.8 %bitcast_add_fusion.1 = f32[4,8,16,720]{3,2,1,0:T(8,128)S(1)} fusion(f32[16,16,1,1]{1,0,3,2:T(8,128)S(1)} %copy-done.12, f32[4,8,16,720]{3,2,1,0:T(8,128)S(1)} %copy-done.3, f32[4,8,720,16]{2,3,1,0:T(8,128)S(1)} %fusion.41, f32[16]{0:T(128)S(1)} %copy-done.16), kind=kOutput, calls=%fused_computation.6 | convolution fusion | flops 72990720 | bytes 4424768 | tf_op jit(solution)/shard_map/nm,rcmw->rcnw/dot_general | solution.py:198
  45.9 1.3 collective-permute-start.4
  47.1 1.2 collective-permute-start.5
  48.3 9.4 %collective-permute-done.4 = f32[1,8,16,720]{3,2,1,0:T(8,128)S(1)} collective-permute-done((f32[1,8,16,720]{3,2,1,0:T(8,128)S(1)}, f32[1,8,16,720]{3,2,1,0:T(8,128)S(1)}, u32[]{:S(2)}, u32[]{:S(2)}) %collective-permute-start.4) | collective-permute-done | bytes 368672 | tf_op jit(solution)/shard_map/ppermute | solution.py:31
  57.7 6.1 %collective-permute-done.5 = f32[1,8,16,720]{3,2,1,0:T(8,128)S(1)} collective-permute-done((f32[1,8,16,720]{3,2,1,0:T(8,128)S(1)}, f32[1,8,16,720]{3,2,1,0:T(8,128)S(1)}, u32[]{:S(2)}, u32[]{:S(2)}) %collective-permute-start.5) | collective-permute-done | bytes 368672 | tf_op jit(solution)/shard_map/ppermute | solution.py:33
  64.5 2.1 %collective-permute-start.6 = (f32[6,1,16,720]{3,2,1,0:T(8,128)S(1)}, f32[6,1,16,720]{3,2,1,0:T(8,128)S(1)}, u32[]{:S(2)}, u32[]{:S(2)}) collective-permute-start(f32[6,1,16,720]{3,2,1,0:T(8,128)S(1)} %get-tuple-element.22), channel_id=1, source_target_pairs={{0,1},{1,2},{2,3},{3,4},{4,5},{5,6},{6,7},{7,0},{8,9},{9,10},{10,1... | collective-permute-start | bytes 829448 | tf_op jit(solution)/shard_map/ppermute | solution.py:31
  67.2 12.1 %all_to_all.19 = s32[32,1,4]{2,1,0:T(1,128)S(1)} all-to-all(s32[32,1,4]{2,1,0:T(1,128)S(1)} %bitcast.75), channel_id=1, replica_groups=mesh['face'=4,'col'=8] {'face','col'}, dimensions={0} | all-to-all | bytes 1024 | tf_op jit(solution)/shard_map/all_to_all | solution.py:217
  81.3 1.9 %pad_maximum_fusion.1 = f32[6,10,16,720]{3,2,1,0:T(8,128)S(1)} fusion(f32[6,1,16,720]{3,2,1,0:T(8,128)} %collective-permute-done.7, f32[1,8,16,720]{3,2,1,0:T(8,128)} %copy-done.8, f32[4,8,16,720]{3,2,1,0:T(8,128)} %copy-done.4, f32[1,8,16,720]{3,2,1,0:T(8,128)S(1)} %collective-permute-done.4, f32[6,1,16,720]{3,2,1,0:T(8,128)} %copy-done.10), kind=kLoop, calls=%fused_computation.3 | loop fusion | flops 2764800 | bytes 5529600 | tf_op jit(solution)/shard_map/concatenate | solution.py:29
  83.2 2.6 %gather_fusion.1 = f32[512,720]{1,0:T(8,128)} fusion(f32[960,720]{1,0:T(8,128)S(1)} %bitcast.69, s32[1024]{0:T(1024)S(1)} %pad_clamp_fusion), kind=kCustom, calls=%fused_computation.1.clone | custom fusion | bytes 2951168 | tf_op jit(solution)/shard_map/jit(_take)/gather | solution.py:202
  85.8 1.7 %broadcast_select_fusion = f32[512,720]{1,0:T(8,128)S(1)} fusion(f32[512,720]{1,0:T(8,128)} %gather_fusion.1, pred[512]{0:T(512)(128)(4,1)S(1)} %compare_and_fusion), kind=kLoop, calls=%fused_computation.11 | loop fusion | flops 368640 | bytes 2949632 | tf_op jit(solution)/shard_map/jit(_take)/select_n | solution.py:202
  87.7 1.6 %fusion = f32[4,8,16,720]{3,2,1,0:T(8,128)S(1)} fusion(f32[4,8,16,720]{3,2,1,0:T(8,128)S(1)} %copy-done.5, f32[4,8,16,720]{3,2,1,0:T(8,128)S(1)} %bitcast.71, f32[16,16,1,1]{1,0,3,2:T(8,128)S(1)} %copy-done.11, f32[16]{0:T(128)S(1)} %copy-done.16), kind=kOutput, calls=%fused_computation.5 | convolution fusion | flops 71516160 | bytes 4424768 | tf_op jit(solution)/shard_map/nm,rcmw->rcnw/dot_general | solution.py:205
  89.3 0.9 convolution_bitcast_fusion
  91.1 2.0 %fusion.42 = f32[128,320]{0,1:T(8,128)S(1)} fusion(f32[128,720]{1,0:T(8,128)S(1)} %reshape.145, f32[720,320]{1,0:T(8,128)S(1)} %copy-done.9), kind=kOutput, calls=%fused_computation.103 | convolution fusion | flops 353894400 | bytes 1454080 | tf_op jit(solution)/shard_map/dot_general | solution.py:223
  94.1 2.8 %all-to-all-start.1 = ((f32[32,4,320]{2,1,0:T(4,128)}), f32[32,4,320]{2,1,0:T(4,128)S(1)}, u32[]{:S(2)}, u32[]{:S(2)}) async-start(f32[32,4,320]{2,1,0:T(4,128)} %reshape.146), calls=%async_computation.1 | async-start | bytes 393216 | tf_op jit(solution)/shard_map/all_to_all | solution.py:224
  97.0 9.3 %all-to-all-done.1 = f32[32,4,320]{2,1,0:T(4,128)S(1)} async-done(((f32[32,4,320]{2,1,0:T(4,128)}), f32[32,4,320]{2,1,0:T(4,128)S(1)}, u32[]{:S(2)}, u32[]{:S(2)}) %all-to-all-start.1) | async-done | bytes 163872 | tf_op jit(solution)/shard_map/all_to_all | solution.py:224
  106.8 2.5 %copy-done = bf16[10,32,64,128]{3,2,1,0:T(8,128)(2,1)S(1)} copy-done((bf16[10,32,64,128]{3,2,1,0:T(8,128)(2,1)S(1)}, bf16[10,32,64,128]{3,2,1,0:T(8,128)(2,1)}, u32[]{:S(2)}) %copy-start) | copy-done | bytes 5242904
  109.3 15.7 %shard_map.121 = (bf16[10,32,64,128]{3,2,1,0:T(8,128)(2,1)}, f32[10,32,128]{2,1,0:T(8,128)S(1)}) custom-call(f32[10,32,128]{2,1,0:T(8,128)S(1)} %fusion.12.force_ref, s32[1,128]{1,0:T(1,128)S(1)} %bitcast.68, bf16[10,32,64,128]{3,2,1,0:T(8,128)(2,1)S(1)} %copy-done), custom_call_target="tpu_custom_call" | custom-call | tf_op jit(solution)/shard_map/pallas_call | solution.py:156
  126.1 2.3 %all-to-all-start.2 = ((f32[32,4,320]{2,1,0:T(4,128)}), f32[32,4,320]{2,1,0:T(4,128)S(1)}, u32[]{:S(2)}, u32[]{:S(2)}) async-start(f32[32,4,320]{2,1,0:T(4,128)} %copy.56), calls=%async_computation.2 | async-start | bytes 393216 | tf_op jit(solution)/shard_map/all_to_all | solution.py:234
  128.8 8.7 %all-to-all-done.2 = f32[32,4,320]{2,1,0:T(4,128)S(1)} async-done(((f32[32,4,320]{2,1,0:T(4,128)}), f32[32,4,320]{2,1,0:T(4,128)S(1)}, u32[]{:S(2)}, u32[]{:S(2)}) %all-to-all-start.2) | async-done | bytes 163872 | tf_op jit(solution)/shard_map/all_to_all | solution.py:234
  137.6 1.0 fusion.4
  (79 shorter events, 8.5 us)
Async XLA Ops:
  4.0 20.4 %copy-start.2 = (f32[4,8,16,720]{3,2,1,0:T(8,128)}, f32[4,8,16,720]{3,2,1,0:T(8,128)S(1)}, u32[]{:S(2)}) copy-start(f32[4,8,16,720]{3,2,1,0:T(8,128)S(1)} %bitcast_add_fusion.3) | copy-start | bytes 4423684
  4.0 3.2 %copy-start.13 = (s32[4,8,4]{1,2,0:T(4,128)S(1)}, s32[4,8,4]{1,2,0:T(4,128)}, u32[]{:S(2)}) copy-start(s32[4,8,4]{1,2,0:T(4,128)} %param.13) | copy-start | bytes 1540
  4.1 11.9 %collective-permute-start = (f32[1,8,16,720]{3,2,1,0:T(8,128)S(1)}, f32[1,8,16,720]{3,2,1,0:T(8,128)S(1)}, u32[]{:S(2)}, u32[]{:S(2)}) collective-permute-start(f32[1,8,16,720]{3,2,1,0:T(8,128)S(1)} %get-tuple-element.28), channel_id=1, source_target_pairs={{0,8},{8,16},{16,24},{24,0},{1,9},{9,17},{17,25},{25,1},{2,10},{10... | collective-permute-start | bytes 1105928 | tf_op jit(solution)/shard_map/ppermute | solution.py:31
  6.2 18.2 %collective-permute-start.1 = (f32[1,8,16,720]{3,2,1,0:T(8,128)S(1)}, f32[1,8,16,720]{3,2,1,0:T(8,128)S(1)}, u32[]{:S(2)}, u32[]{:S(2)}) collective-permute-start(f32[1,8,16,720]{3,2,1,0:T(8,128)S(1)} %get-tuple-element.29), channel_id=1, source_target_pairs={{8,0},{16,8},{24,16},{0,24},{9,1},{17,9},{25,17},{1,25},{10,2},{18... | collective-permute-start | bytes 1105928 | tf_op jit(solution)/shard_map/ppermute | solution.py:33
  24.3 7.1 %copy-start.7 = (f32[1,8,16,720]{3,2,1,0:T(8,128)}, f32[1,8,16,720]{3,2,1,0:T(8,128)S(1)}, u32[]{:S(2)}) copy-start(f32[1,8,16,720]{3,2,1,0:T(8,128)S(1)} %collective-permute-done.1) | copy-start | bytes 1105924
  24.4 7.0 %collective-permute-start.2 = (f32[6,1,16,720]{3,2,1,0:T(8,128)S(1)}, f32[6,1,16,720]{3,2,1,0:T(8,128)S(1)}, u32[]{:S(2)}, u32[]{:S(2)}) collective-permute-start(f32[6,1,16,720]{3,2,1,0:T(8,128)S(1)} %get-tuple-element.24), channel_id=1, source_target_pairs={{0,1},{1,2},{2,3},{3,4},{4,5},{5,6},{6,7},{7,0},{8,9},{9,10},{10,1... | collective-permute-start | bytes 829448 | tf_op jit(solution)/shard_map/ppermute | solution.py:31
  27.2 9.2 %collective-permute-start.3 = (f32[6,1,16,720]{3,2,1,0:T(8,128)S(1)}, f32[6,1,16,720]{3,2,1,0:T(8,128)S(1)}, u32[]{:S(2)}, u32[]{:S(2)}) collective-permute-start(f32[6,1,16,720]{3,2,1,0:T(8,128)S(1)} %get-tuple-element.25), channel_id=1, source_target_pairs={{1,0},{2,1},{3,2},{4,3},{5,4},{6,5},{7,6},{0,7},{9,8},{10,9},{11,1... | collective-permute-start | bytes 829448 | tf_op jit(solution)/shard_map/ppermute | solution.py:33
  40.8 1.6 %copy-start.11 = (f32[16,16,1,1]{1,0,3,2:T(8,128)S(1)}, f32[16,16,1,1]{1,0,3,2:T(8,128)}, u32[]{:S(2)}) copy-start(f32[16,16,1,1]{1,0,3,2:T(8,128)} %constant.151) | copy-start | bytes 3076
  42.4 1.5 %copy-start.3 = (f32[4,8,16,720]{3,2,1,0:T(8,128)S(1)}, f32[4,8,16,720]{3,2,1,0:T(8,128)}, u32[]{:S(2)}) copy-start(f32[4,8,16,720]{3,2,1,0:T(8,128)} %copy-done.2) | copy-start | bytes 4423684
  42.4 1.5 %copy-start.12 = (f32[16,16,1,1]{1,0,3,2:T(8,128)S(1)}, f32[16,16,1,1]{1,0,3,2:T(8,128)}, u32[]{:S(2)}) copy-start(f32[16,16,1,1]{1,0,3,2:T(8,128)} %constant.150) | copy-start | bytes 3076
  42.5 1.5 %copy-start.16 = (f32[16]{0:T(128)S(1)}, f32[16]{0:T(128)}, u32[]{:S(2)}) copy-start(f32[16]{0:T(128)} %constant.148) | copy-start | bytes 196
  45.8 18.0 %copy-start.4 = (f32[4,8,16,720]{3,2,1,0:T(8,128)}, f32[4,8,16,720]{3,2,1,0:T(8,128)S(1)}, u32[]{:S(2)}) copy-start(f32[4,8,16,720]{3,2,1,0:T(8,128)S(1)} %bitcast_add_fusion.1) | copy-start | bytes 4423684
  45.9 20.7 %copy-start.14 = (s32[4,8,4]{1,2,0:T(4,128)S(1)}, s32[4,8,4]{1,2,0:T(4,128)}, u32[]{:S(2)}) copy-start(s32[4,8,4]{1,2,0:T(4,128)} %param.14) | copy-start | bytes 1540
  45.9 11.8 %collective-permute-start.4 = (f32[1,8,16,720]{3,2,1,0:T(8,128)S(1)}, f32[1,8,16,720]{3,2,1,0:T(8,128)S(1)}, u32[]{:S(2)}, u32[]{:S(2)}) collective-permute-start(f32[1,8,16,720]{3,2,1,0:T(8,128)S(1)} %get-tuple-element.26), channel_id=1, source_target_pairs={{0,8},{8,16},{16,24},{24,0},{1,9},{9,17},{17,25},{25,1},{2,10},{10... | collective-permute-start | bytes 1105928 | tf_op jit(solution)/shard_map/ppermute | solution.py:31
  47.1 16.6 %collective-permute-start.5 = (f32[1,8,16,720]{3,2,1,0:T(8,128)S(1)}, f32[1,8,16,720]{3,2,1,0:T(8,128)S(1)}, u32[]{:S(2)}, u32[]{:S(2)}) collective-permute-start(f32[1,8,16,720]{3,2,1,0:T(8,128)S(1)} %get-tuple-element.27), channel_id=1, source_target_pairs={{8,0},{16,8},{24,16},{0,24},{9,1},{17,9},{25,17},{1,25},{10,2},{18... | collective-permute-start | bytes 1105928 | tf_op jit(solution)/shard_map/ppermute | solution.py:33
  63.8 0.7 copy-start.8
  64.5 16.1 %collective-permute-start.6 = (f32[6,1,16,720]{3,2,1,0:T(8,128)S(1)}, f32[6,1,16,720]{3,2,1,0:T(8,128)S(1)}, u32[]{:S(2)}, u32[]{:S(2)}) collective-permute-start(f32[6,1,16,720]{3,2,1,0:T(8,128)S(1)} %get-tuple-element.22), channel_id=1, source_target_pairs={{0,1},{1,2},{2,3},{3,4},{4,5},{5,6},{6,7},{7,0},{8,9},{9,10},{10,1... | collective-permute-start | bytes 829448 | tf_op jit(solution)/shard_map/ppermute | solution.py:31
  66.6 14.7 %collective-permute-start.7 = (f32[6,1,16,720]{3,2,1,0:T(8,128)S(1)}, f32[6,1,16,720]{3,2,1,0:T(8,128)}, u32[]{:S(2)}, u32[]{:S(2)}) collective-permute-start(f32[6,1,16,720]{3,2,1,0:T(8,128)S(1)} %get-tuple-element.23), channel_id=1, source_target_pairs={{1,0},{2,1},{3,2},{4,3},{5,4},{6,5},{7,6},{0,7},{9,8},{10,9},{11,1... | collective-permute-start | bytes 829448 | tf_op jit(solution)/shard_map/ppermute | solution.py:33
  80.6 0.7 copy-start.10
  85.8 1.9 %copy-start.5 = (f32[4,8,16,720]{3,2,1,0:T(8,128)S(1)}, f32[4,8,16,720]{3,2,1,0:T(8,128)}, u32[]{:S(2)}) copy-start(f32[4,8,16,720]{3,2,1,0:T(8,128)} %copy-done.4) | copy-start | bytes 4423684
  87.7 1.6 %copy-start.15 = (f32[4,16,1,1]{1,0,3,2:T(4,128)S(1)}, f32[4,16,1,1]{1,0,3,2:T(4,128)}, u32[]{:S(2)}) copy-start(f32[4,16,1,1]{1,0,3,2:T(4,128)} %constant.152) | copy-start | bytes 772
  89.3 3.8 %copy-start.6 = (f32[4,8,16,720]{3,2,1,0:T(8,128)}, f32[4,8,16,720]{3,2,1,0:T(8,128)S(1)}, u32[]{:S(2)}) copy-start(f32[4,8,16,720]{3,2,1,0:T(8,128)S(1)} %fusion) | copy-start | bytes 4423684
  89.3 1.8 %copy-start.9 = (f32[720,320]{1,0:T(8,128)S(1)}, f32[720,320]{1,0:T(8,128)}, u32[]{:S(2)}) copy-start(f32[720,320]{1,0:T(8,128)} %constant.147.clone) | copy-start | bytes 2764804
  91.1 15.7 %copy-start.1 = (s32[128]{0:T(128)S(1)}, s32[128]{0:T(128)}, u32[]{:S(2)}) copy-start(s32[128]{0:T(128)} %param.15) | copy-start | bytes 1540
  94.1 12.2 %all-to-all-start.1 = ((f32[32,4,320]{2,1,0:T(4,128)}), f32[32,4,320]{2,1,0:T(4,128)S(1)}, u32[]{:S(2)}, u32[]{:S(2)}) async-start(f32[32,4,320]{2,1,0:T(4,128)} %reshape.146), calls=%async_computation.1 | async-start | bytes 393216 | tf_op jit(solution)/shard_map/all_to_all | solution.py:224
  106.8 2.5 %copy-start = (bf16[10,32,64,128]{3,2,1,0:T(8,128)(2,1)S(1)}, bf16[10,32,64,128]{3,2,1,0:T(8,128)(2,1)}, u32[]{:S(2)}) copy-start(bf16[10,32,64,128]{3,2,1,0:T(8,128)(2,1)} %state_hbm.1) | copy-start | bytes 15728644
  126.1 11.4 %all-to-all-start.2 = ((f32[32,4,320]{2,1,0:T(4,128)}), f32[32,4,320]{2,1,0:T(4,128)S(1)}, u32[]{:S(2)}, u32[]{:S(2)}) async-start(f32[32,4,320]{2,1,0:T(4,128)} %copy.56), calls=%async_computation.2 | async-start | bytes 393216 | tf_op jit(solution)/shard_map/all_to_all | solution.py:234

commit v2 on v1

--- a/solution.py
+++ b/solution.py
@@ -1,3 +1,5 @@
+import functools
+
 import jax
 import jax.numpy as jnp
 import numpy as np
@@ -19,22 +21,6 @@
 DIFF_Z = 0.1
 RELAX = 0.2
 CONVERT = 0.5
-
-
-def extended_2(cells, sides, width):
-    for axis, dim in sides:
-        count = lax.axis_size(axis)
-        head = lax.slice_in_dim(cells, 0, width, axis=dim)
-        tail = lax.slice_in_dim(cells, cells.shape[dim] - width, cells.shape[dim], axis=dim)
-        cells = jnp.concatenate(
-            [
-                lax.ppermute(tail, axis, [(i, (i + 1) % count) for i in range(count)]),
-                cells,
-                lax.ppermute(head, axis, [((i + 1) % count, i) for i in range(count)]),
-            ],
-            axis=dim,
-        )
-    return cells
 
 
 def node_tables():
@@ -68,6 +54,118 @@
     base = jnp.where(other_edge == 1, 3, jnp.where(other_edge == 2, 12, 0))
     stride = jnp.where((other_edge == 1) | (other_edge == 3), 4, 1)
     return base[..., None] + stride[..., None] * along
+
+
+DIRECTIONS = tuple((a, b) for a in (-1, 0, 1) for b in (-1, 0, 1) if (a, b) != (0, 0))
+EDGE_NODES = ((0, 1, 2, 3), (3, 7, 11, 15), (12, 13, 14, 15), (0, 4, 8, 12))
+
+
+def dyn_kernel(
+    nface, ncol, row_ref, col_ref, point_ref, state_ref, out_ref, ext0, ext1, gathered, send_sem, recv_sem
+):
+    rows, cols, nodes, width = state_ref.shape
+    face, col = lax.axis_index("face"), lax.axis_index("col")
+    lanes = cols * nodes
+
+    def device(direction):
+        return (
+            lax.rem(face + direction[0] + nface, nface),
+            lax.rem(col + direction[1] + ncol, ncol),
+        )
+
+    barrier = pltpu.get_barrier_semaphore()
+    for direction in DIRECTIONS:
+        pl.semaphore_signal(
+            barrier, inc=1, device_id=device(direction), device_id_type=pl.DeviceIdType.MESH
+        )
+    pl.semaphore_wait(barrier, len(DIRECTIONS))
+
+    def taken(step, size):
+        return {-1: 1, 0: pl.ds(1, size), 1: size}[step]
+
+    def landed(step, size):
+        return {-1: size + 1, 0: pl.ds(1, size), 1: 0}[step]
+
+    def copy(ext, step, i):
+        a, b = DIRECTIONS[i]
+        return pltpu.make_async_remote_copy(
+            src_ref=ext.at[taken(a, rows), taken(b, cols)],
+            dst_ref=ext.at[landed(a, rows), landed(b, cols)],
+            send_sem=send_sem.at[step, i],
+            recv_sem=recv_sem.at[step, i],
+            device_id=device(DIRECTIONS[i]),
+            device_id_type=pl.DeviceIdType.MESH,
+        )
+
+    node = lax.rem(lax.broadcasted_iota(jnp.int32, (lanes, 1), 0), nodes)
+    na, nb = lax.div(node, 4), lax.rem(node, 4)
+    weights = [
+        jnp.where(mask, KAPPA, 0.0) for mask in (na > 0, na < 3, nb > 0, nb < 3)
+    ]
+    own = 1.0 - (weights[0] + weights[1] + weights[2] + weights[3])
+    ends = jnp.where((na == 0) | (na == 3), 1.0, 0.0) + jnp.where((nb == 0) | (nb == 3), 1.0, 0.0)
+    share = 1.0 / (1.0 + ends)
+    shifts = (4, lanes - 4, 1, lanes - 1)
+
+    for r in range(rows):
+        gathered[r] = jnp.zeros((cols, nodes, width), jnp.float32)
+
+    for step in range(DSTEPS):
+        src, ext = (state_ref, ext0) if step == 0 else (out_ref, ext1)
+        for r in (0, rows - 1) + tuple(range(1, rows - 1)):
+            flat = src[r].reshape(lanes, width)
+            smooth = own * flat
+            for weight, shift in zip(weights, shifts):
+                smooth = smooth + weight * pltpu.roll(flat, shift, 0)
+            ext[r + 1, 1 : cols + 1] = smooth.reshape(cols, nodes, width)
+        copies = [copy(ext, step, i) for i in range(len(DIRECTIONS))]
+        for one in copies:
+            one.start()
+        for one in copies:
+            one.wait_recv()
+
+        @pl.loop(0, rows * cols)
+        def _(e):
+            r, c = lax.div(e, cols), lax.rem(e, cols)
+            terms = {}
+            for k in range(4):
+                for i in range(4):
+                    at = e * 16 + k * 4 + i
+                    value = ext[row_ref[at], col_ref[at], pl.ds(point_ref[at], 1), :]
+                    terms.setdefault(EDGE_NODES[k][i], []).append(value)
+            for p, values in terms.items():
+                total = values[0] if len(values) == 1 else values[0] + values[1]
+                gathered[r, c, p : p + 1, :] = total
+
+        for r in range(rows):
+            flat = ext[r + 1, 1 : cols + 1].reshape(lanes, width)
+            fresh = (flat + gathered[r].reshape(lanes, width)) * share
+            out_ref[r] = fresh.reshape(cols, nodes, width)
+        for one in copies:
+            one.wait_send()
+
+
+def dyn_run(state, near_row, near_col, point):
+    rows, cols, nodes, width = state.shape
+    vmem = pl.BlockSpec(memory_space=pltpu.VMEM)
+    smem = pl.BlockSpec(memory_space=pltpu.SMEM)
+    halo = pltpu.VMEM((rows + 2, cols + 2, nodes, width), jnp.float32)
+    return pl.pallas_call(
+        functools.partial(dyn_kernel, lax.axis_size("face"), lax.axis_size("col")),
+        out_shape=jax.ShapeDtypeStruct(state.shape, jnp.float32),
+        in_specs=[smem, smem, smem, vmem],
+        out_specs=vmem,
+        scratch_shapes=[
+            halo,
+            halo,
+            pltpu.VMEM(state.shape, jnp.float32),
+            pltpu.SemaphoreType.DMA((DSTEPS, len(DIRECTIONS))),
+            pltpu.SemaphoreType.DMA((DSTEPS, len(DIRECTIONS))),
+        ],
+        compiler_params=pltpu.CompilerParams(
+            collective_id=0, has_side_effects=True, vmem_limit_bytes=32 * 2**20
+        ),
+    )(near_row, near_col, point, state)
 
 
 def crm_kernel(force_ref, active_ref, state_hbm, out_hbm, tend_ref, held, first, final, begin, in_sem, out_sem):
@@ -190,20 +288,13 @@
     local_col = lax.broadcasted_iota(jnp.int32, (rows_dev, cols_dev, 4), 1)
     drow = (near_row - (lax.axis_index("face") * rows_dev + local_row) + 1) % total_rows - 1
     dcol = (near_col - (lax.axis_index("col") * cols_dev + local_col) + 1) % total_cols - 1
-    place = (local_row + drow + 1) * (cols_dev + 2) + (local_col + dcol + 1)
-    index_flat = place[..., None] * 16 + pick
-    index_flat = index_flat.reshape(-1)
-    state = dyn_state
-    for step in range(DSTEPS):
-        state = state + KAPPA * jnp.einsum(
-            "nm,rcmw->rcnw", laplace, state, precision=lax.Precision.HIGHEST
-        )
-        extended = extended_2(state, (("face", 0), ("col", 1)), 1)
-        matched = jnp.take(extended.reshape(-1, width), index_flat, axis=0).reshape(
-            rows_dev, cols_dev, 16, width
-        )
-        summed = jnp.einsum("nm,rcmw->rcnw", spread, matched, precision=lax.Precision.HIGHEST)
-        state = (state + summed) / denom[None, None, :, None]
+    shape = pick.shape
+    state = dyn_run(
+        dyn_state,
+        jnp.broadcast_to((local_row + drow + 1)[..., None], shape).reshape(-1),
+        jnp.broadcast_to((local_col + dcol + 1)[..., None], shape).reshape(-1),
+        pick.reshape(-1),
+    )
     columns = jnp.einsum("qn,rcnw->rcqw", quarter, state, precision=exact).reshape(-1, width)
     per_dev = columns.shape[0]
     count = per_dev // ndev
@@ -214,21 +305,19 @@
     rank = jnp.sum((keys_local[None, :] < keys_local[:, None]).astype(jnp.int32), axis=1)
     sorting = rank[None, :] == jnp.arange(per_dev, dtype=jnp.int32)[:, None]
     out_keys = jnp.sum(jnp.where(sorting, keys_local[None, :], 0), axis=1)
-    arrived_keys = lax.all_to_all(
-        out_keys.reshape(ndev, count), ("face", "col"), split_axis=0, concat_axis=0, tiled=True
-    )
-    slots = arrived_keys.reshape(-1) % per_dev
-    landing = (slots[:, None] == jnp.arange(per_dev, dtype=jnp.int32)[None, :]).astype(jnp.float32)
     sorting = sorting.astype(jnp.float32)
     outgoing = jnp.dot(sorting, jnp.dot(columns, keep, precision=exact), precision=exact)
+    outgoing = jnp.concatenate([outgoing, out_keys[:, None].astype(jnp.float32)], axis=1)
     arrived = lax.all_to_all(
-        outgoing.reshape(ndev, count, depth),
+        outgoing.reshape(ndev, count, depth + 1),
         ("face", "col"),
         split_axis=0,
         concat_axis=0,
         tiled=True,
-    )
-    forcing = jnp.einsum("sw,sc->wc", arrived.reshape(per_dev, depth), landing, precision=exact)
+    ).reshape(per_dev, depth + 1)
+    slots = arrived[:, depth].astype(jnp.int32) % per_dev
+    landing = (slots[:, None] == jnp.arange(per_dev, dtype=jnp.int32)[None, :]).astype(jnp.float32)
+    forcing = jnp.einsum("sw,sc->wc", arrived[:, :depth], landing, precision=exact)
     crm_new, tend = crm_run(crm_state, forcing.reshape(NFLD, CLEV, per_dev), crm_active)
     tend_rows = jnp.einsum("sc,wc->sw", landing, tend.reshape(depth, per_dev), precision=exact)
     returned = lax.all_to_all(

time: 139 us -> 115 us (0.83)
  Pallas kernels: 15.7 us -> 73.2 us
  waiting for transfers between devices: 59 us -> 8.84 us
  starting transfers between devices: 15.5 us -> 2.32 us
  matrix products: 13 us -> 4.8 us
  other arithmetic: 8.49 us -> 2.36 us
  local copies, waits for them, and re-layouts: 13.8 us -> 8.92 us
    pallas_call x0 -> x1, Pallas kernels: none -> 57.5 us  [dyn_run(): pl.pallas_call(functools.partial(dyn_kernel, lax.axis_size('face'), lax.a...]
    ppermute x8 -> x0, waiting for transfers between devices: 40.9 us -> none  [the longest x4 21.4 us: extended_2(): lax.ppermute(tail, axis, [(i, (i + 1) % count) for i in range(count)])]
    ppermute x8 -> x0, starting transfers between devices: 10.4 us -> none  [the longest x4 8.2 us: extended_2(): lax.ppermute(tail, axis, [(i, (i + 1) % count) for i in range(count)])]
    all_to_all x1 -> x0, waiting for transfers between devices: 9.33 us -> none  [per_device(): lax.all_to_all(outgoing.reshape(ndev, count, depth), ('face', 'col'), spl...]
    dot_general x5 -> x1, matrix products: 8.52 us -> 0.37 us  [per_device(): jnp.einsum('sw,sc->wc', arrived[:, :depth], landing, precision=exact)]
    gather x2 -> x0, local copies, waits for them, and re-layouts: 5.19 us -> none  [per_device(): jnp.take(extended.reshape(-1, width), index_flat, axis=0)]
    concatenate x2 -> x1, other arithmetic: 3.69 us -> 0.1 us  [per_device(): jnp.concatenate([outgoing, out_keys[:, None].astype(jnp.float32)], axis=1)]
    select_n x5 -> x1, other arithmetic: 3.31 us -> 0.18 us  [per_device(): slots = arrived[:, depth].astype(jnp.int32) % per_dev]
  transfers between devices with their start and end apart: 10 -> 1, of which waited for: 8 -> 1; matrix products, arithmetic and copies ran while one was open for 2% -> 0% of each run, Pallas kernels for 0% -> 0%
where the time goes in v2:
time: 115 us; the launch traced here: 114 us
  Pallas kernels  73.2 us (64%)
  blocking collectives  12.9 us (11%)
  local copies, waits for them, and re-layouts  8.92 us (8%)
  waiting for transfers between devices  8.84 us (8%)
  matrix products  4.8 us (4%)
  other arithmetic  2.36 us (2%)
  starting transfers between devices  2.32 us (2%)
    pallas_call x1, Pallas kernels, dyn_run(): pl.pallas_call(functools.partial(dyn_kernel, lax.axis_size('face'), lax.a...  57.5 us
    pallas_call x1, Pallas kernels, crm_run(): pl.pallas_call(crm_kernel, out_shape=(jax.ShapeDtypeStruct(state.shape, s...  15.7 us
    all_to_all x1, blocking collectives, per_device(): lax.all_to_all(outgoing.reshape(ndev, count, depth + 1), ('face', 'col'),...  12.9 us
    all_to_all x1, waiting for transfers between devices, per_device(): lax.all_to_all(tend_rows.reshape(ndev, count, depth), ('face', 'col'), sp...  8.84 us
    unnamed x12, local copies, waits for them, and re-layouts  6 us
    all_to_all x1, starting transfers between devices, per_device(): lax.all_to_all(tend_rows.reshape(ndev, count, depth), ('face', 'col'), sp...  2.32 us
  transfers between devices with their start and end apart: 1, of which 1 were waited for; matrix products, arithmetic and copies ran while one was open for 0% of the time, Pallas kernels for 0%

profile of v2, /device:TPU:1, one launch (start us, length us, event | category | flops | bytes accessed | tf_op | source)
XLA Modules:
  0.0 114.3 jit_solution(11565578894755499630)
XLA Ops:
  0.7 0.7 fusion.29
  1.4 0.8 select_select_fusion
  2.2 0.1 copy.58
  2.4 0.1 reshape.106.row_ref
  2.7 0.1 reshape.107.col_ref
  3.0 0.1 copy.62
  3.2 0.2 multiply_add_fusion
  3.3 0.1 add.95.point_ref
  3.4 0.8 copy.63
  4.2 0.1 lt.48
  4.3 0.2 convert_reduce_fusion
  4.5 0.1 select_reduce_fusion
  4.7 0.3 convert_element_type.28
  4.9 1.4 %copy-done.1 = f32[4,8,16,720]{3,2,1,0:T(8,128)S(1)} copy-done((f32[4,8,16,720]{3,2,1,0:T(8,128)S(1)}, f32[4,8,16,720]{3,2,1,0:T(8,128)}, u32[]{:S(2)}) %copy-start.1) | copy-done | bytes 1474584
  6.3 57.5 %shard_map.94 = f32[4,8,16,720]{3,2,1,0:T(8,128)S(1)} custom-call(s32[512]{0:T(512)S(1)} %reshape.106.row_ref, s32[512]{0:T(512)S(1)} %reshape.107.col_ref, s32[512]{0:T(512)S(1)} %add.95.point_ref, f32[4,8,16,720]{3,2,1,0:T(8,128)S(1)} %copy-done.1), custom_call_target="tpu_custom_call" | custom-call | tf_op jit(solution)/shard_map/pallas_call | solution.py:153
  63.9 0.9 convolution_bitcast_fusion
  64.9 0.1 reshape.108
  65.0 0.1 copy-done.3
  65.1 2.0 %fusion.31 = f32[128,320]{0,1:T(8,128)S(1)} fusion(f32[128,720]{1,0:T(8,128)S(1)} %reshape.108, f32[720,320]{1,0:T(8,128)S(1)} %copy-done.3), kind=kOutput, calls=%fused_computation.75 | convolution fusion | flops 353894400 | bytes 1454080 | tf_op jit(solution)/shard_map/dot_general | solution.py:309
  67.1 0.3 fusion.6
  67.5 0.1 pad_maximum_fusion
  67.6 12.9 %all_to_all.10 = f32[32,4,321]{2,1,0:T(4,128)S(1)} all-to-all(f32[32,4,321]{2,1,0:T(4,128)S(1)} %pad_maximum_fusion), channel_id=1, replica_groups=mesh['face'=4,'col'=8] {'face','col'}, dimensions={0} | all-to-all | bytes 328704 | tf_op jit(solution)/shard_map/all_to_all | solution.py:311
  80.5 0.2 fusion.5
  80.7 0.4 fusion
  81.3 2.5 %copy-done = bf16[10,32,64,128]{3,2,1,0:T(8,128)(2,1)S(1)} copy-done((bf16[10,32,64,128]{3,2,1,0:T(8,128)(2,1)S(1)}, bf16[10,32,64,128]{3,2,1,0:T(8,128)(2,1)}, u32[]{:S(2)}) %copy-start) | copy-done | bytes 5242904
  83.8 15.7 %shard_map.95 = (bf16[10,32,64,128]{3,2,1,0:T(8,128)(2,1)}, f32[10,32,128]{2,1,0:T(8,128)S(1)}) custom-call(f32[10,32,128]{2,1,0:T(8,128)S(1)} %bitcast.24, s32[1,128]{1,0:T(1,128)S(1)} %bitcast.26, bf16[10,32,64,128]{3,2,1,0:T(8,128)(2,1)S(1)} %copy-done), custom_call_target="tpu_custom_call" | custom-call | tf_op jit(solution)/shard_map/pallas_call | solution.py:254
  99.5 0.3 fusion.9
  99.8 0.8 copy.68
  100.6 2.3 %all-to-all-start.1 = ((f32[32,4,320]{2,1,0:T(4,128)}), f32[32,4,320]{2,1,0:T(4,128)S(1)}, u32[]{:S(2)}, u32[]{:S(2)}) async-start(f32[32,4,320]{2,1,0:T(4,128)} %copy.68), calls=%async_computation.1 | async-start | bytes 393216 | tf_op jit(solution)/shard_map/all_to_all | solution.py:323
  103.2 8.8 %all-to-all-done.1 = f32[32,4,320]{2,1,0:T(4,128)S(1)} async-done(((f32[32,4,320]{2,1,0:T(4,128)}), f32[32,4,320]{2,1,0:T(4,128)S(1)}, u32[]{:S(2)}, u32[]{:S(2)}) %all-to-all-start.1) | async-done | bytes 163872 | tf_op jit(solution)/shard_map/all_to_all | solution.py:323
  112.2 1.0 fusion.2
  113.1 1.1 copy.80
  (25 shorter events, 1.2 us)
Async XLA Ops:
  4.9 1.4 %copy-start.1 = (f32[4,8,16,720]{3,2,1,0:T(8,128)S(1)}, f32[4,8,16,720]{3,2,1,0:T(8,128)}, u32[]{:S(2)}) copy-start(f32[4,8,16,720]{3,2,1,0:T(8,128)} %state_ref.1) | copy-start | bytes 4423684
  6.3 57.6 %copy-start.4 = (f32[4,16,1,1]{1,0,3,2:T(4,128)S(1)}, f32[4,16,1,1]{1,0,3,2:T(4,128)}, u32[]{:S(2)}) copy-start(f32[4,16,1,1]{1,0,3,2:T(4,128)} %constant.124) | copy-start | bytes 772
  63.9 1.2 %copy-start.3 = (f32[720,320]{1,0:T(8,128)S(1)}, f32[720,320]{1,0:T(8,128)}, u32[]{:S(2)}) copy-start(f32[720,320]{1,0:T(8,128)} %constant.123.clone) | copy-start | bytes 2764804
  67.1 14.2 %copy-start.2 = (s32[128]{0:T(128)S(1)}, s32[128]{0:T(128)}, u32[]{:S(2)}) copy-start(s32[128]{0:T(128)} %param.10) | copy-start | bytes 1540
  81.3 2.5 %copy-start = (bf16[10,32,64,128]{3,2,1,0:T(8,128)(2,1)S(1)}, bf16[10,32,64,128]{3,2,1,0:T(8,128)(2,1)}, u32[]{:S(2)}) copy-start(bf16[10,32,64,128]{3,2,1,0:T(8,128)(2,1)} %state_hbm.1) | copy-start | bytes 15728644
  100.6 11.5 %all-to-all-start.1 = ((f32[32,4,320]{2,1,0:T(4,128)}), f32[32,4,320]{2,1,0:T(4,128)S(1)}, u32[]{:S(2)}, u32[]{:S(2)}) async-start(f32[32,4,320]{2,1,0:T(4,128)} %copy.68), calls=%async_computation.1 | async-start | bytes 393216 | tf_op jit(solution)/shard_map/all_to_all | solution.py:323

commit v3 on v2

--- a/solution.py
+++ b/solution.py
@@ -53,55 +53,68 @@
     along = jnp.where(reversal[..., None] == 1, 3 - points, points)
     base = jnp.where(other_edge == 1, 3, jnp.where(other_edge == 2, 12, 0))
     stride = jnp.where((other_edge == 1) | (other_edge == 3), 4, 1)
-    return base[..., None] + stride[..., None] * along
-
-
-DIRECTIONS = tuple((a, b) for a in (-1, 0, 1) for b in (-1, 0, 1) if (a, b) != (0, 0))
+    point = base[..., None] + stride[..., None] * along
+    skipped = sum(jnp.where(point > inner, 1, 0) for inner in (5, 6, 9, 10))
+    return point - skipped
+
+
+SIDES = ((-1, 0), (1, 0), (0, -1), (0, 1))
 EDGE_NODES = ((0, 1, 2, 3), (3, 7, 11, 15), (12, 13, 14, 15), (0, 4, 8, 12))
+RIM = (0, 1, 2, 3, 4, 7, 8, 11, 12, 13, 14, 15)
+SIDE = 16
+RUNS = ((0, 0, 5), (5, 7, 2), (7, 11, 5))
 
 
 def dyn_kernel(
-    nface, ncol, row_ref, col_ref, point_ref, state_ref, out_ref, ext0, ext1, gathered, send_sem, recv_sem
+    nface, ncol, row_ref, point_ref, state_ref, out_ref, ext0, ext1, smoothed, gathered, send_sem, recv_sem
 ):
     rows, cols, nodes, width = state_ref.shape
     face, col = lax.axis_index("face"), lax.axis_index("col")
     lanes = cols * nodes
-
-    def device(direction):
+    rim = len(RIM)
+    own_cols = pl.ds(SIDE, cols * rim)
+    first_col, last_col = pl.ds(SIDE, SIDE), pl.ds(cols * rim, SIDE)
+    west_halo, east_halo = pl.ds(0, SIDE), pl.ds(SIDE + cols * rim, SIDE)
+    own_rows = pl.ds(1, rows)
+
+    def device(side):
         return (
-            lax.rem(face + direction[0] + nface, nface),
-            lax.rem(col + direction[1] + ncol, ncol),
+            lax.rem(face + side[0] + nface, nface),
+            lax.rem(col + side[1] + ncol, ncol),
         )
 
     barrier = pltpu.get_barrier_semaphore()
-    for direction in DIRECTIONS:
+    for side in SIDES:
         pl.semaphore_signal(
-            barrier, inc=1, device_id=device(direction), device_id_type=pl.DeviceIdType.MESH
-        )
-    pl.semaphore_wait(barrier, len(DIRECTIONS))
-
-    def taken(step, size):
-        return {-1: 1, 0: pl.ds(1, size), 1: size}[step]
-
-    def landed(step, size):
-        return {-1: size + 1, 0: pl.ds(1, size), 1: 0}[step]
+            barrier, inc=1, device_id=device(side), device_id_type=pl.DeviceIdType.MESH
+        )
+    pl.semaphore_wait(barrier, len(SIDES))
+
+    plan = (
+        ((1, own_cols), (rows + 1, own_cols), SIDES[0]),
+        ((rows, own_cols), (0, own_cols), SIDES[1]),
+        ((own_rows, first_col), (own_rows, east_halo), SIDES[2]),
+        ((own_rows, last_col), (own_rows, west_halo), SIDES[3]),
+        ((rows + 1, first_col), (rows + 1, east_halo), SIDES[2]),
+        ((rows + 1, last_col), (rows + 1, west_halo), SIDES[3]),
+        ((0, first_col), (0, east_halo), SIDES[2]),
+        ((0, last_col), (0, west_halo), SIDES[3]),
+    )
 
     def copy(ext, step, i):
-        a, b = DIRECTIONS[i]
+        here, there, side = plan[i]
         return pltpu.make_async_remote_copy(
-            src_ref=ext.at[taken(a, rows), taken(b, cols)],
-            dst_ref=ext.at[landed(a, rows), landed(b, cols)],
+            src_ref=ext.at[here],
+            dst_ref=ext.at[there],
             send_sem=send_sem.at[step, i],
             recv_sem=recv_sem.at[step, i],
-            device_id=device(DIRECTIONS[i]),
+            device_id=device(side),
             device_id_type=pl.DeviceIdType.MESH,
         )
 
     node = lax.rem(lax.broadcasted_iota(jnp.int32, (lanes, 1), 0), nodes)
     na, nb = lax.div(node, 4), lax.rem(node, 4)
-    weights = [
-        jnp.where(mask, KAPPA, 0.0) for mask in (na > 0, na < 3, nb > 0, nb < 3)
-    ]
+    weights = [jnp.where(mask, KAPPA, 0.0) for mask in (na > 0, na < 3, nb > 0, nb < 3)]
     own = 1.0 - (weights[0] + weights[1] + weights[2] + weights[3])
     ends = jnp.where((na == 0) | (na == 3), 1.0, 0.0) + jnp.where((nb == 0) | (nb == 3), 1.0, 0.0)
     share = 1.0 / (1.0 + ends)
@@ -112,16 +125,29 @@
 
     for step in range(DSTEPS):
         src, ext = (state_ref, ext0) if step == 0 else (out_ref, ext1)
+        copies = [copy(ext, step, i) for i in range(len(plan))]
         for r in (0, rows - 1) + tuple(range(1, rows - 1)):
             flat = src[r].reshape(lanes, width)
             smooth = own * flat
             for weight, shift in zip(weights, shifts):
                 smooth = smooth + weight * pltpu.roll(flat, shift, 0)
-            ext[r + 1, 1 : cols + 1] = smooth.reshape(cols, nodes, width)
-        copies = [copy(ext, step, i) for i in range(len(DIRECTIONS))]
-        for one in copies:
+            smoothed[r] = smooth.reshape(cols, nodes, width)
+            for c in range(cols):
+                for to, at, size in RUNS:
+                    ext[r + 1, pl.ds(SIDE + c * rim + to, size), :] = smoothed[r, c, pl.ds(at, size), :]
+            if r == 0:
+                copies[0].start()
+            if r == rows - 1:
+                copies[1].start()
+        copies[2].start()
+        copies[3].start()
+        copies[0].wait_recv()
+        copies[4].start()
+        copies[5].start()
+        copies[1].wait_recv()
+        for one in copies[6:]:
             one.start()
-        for one in copies:
+        for one in copies[2:]:
             one.wait_recv()
 
         @pl.loop(0, rows * cols)
@@ -131,41 +157,42 @@
             for k in range(4):
                 for i in range(4):
                     at = e * 16 + k * 4 + i
-                    value = ext[row_ref[at], col_ref[at], pl.ds(point_ref[at], 1), :]
+                    value = ext[row_ref[at], pl.ds(point_ref[at], 1), :]
                     terms.setdefault(EDGE_NODES[k][i], []).append(value)
             for p, values in terms.items():
                 total = values[0] if len(values) == 1 else values[0] + values[1]
                 gathered[r, c, p : p + 1, :] = total
 
         for r in range(rows):
-            flat = ext[r + 1, 1 : cols + 1].reshape(lanes, width)
-            fresh = (flat + gathered[r].reshape(lanes, width)) * share
-            out_ref[r] = fresh.reshape(cols, nodes, width)
+            out_ref[r] = (
+                (smoothed[r].reshape(lanes, width) + gathered[r].reshape(lanes, width)) * share
+            ).reshape(cols, nodes, width)
         for one in copies:
             one.wait_send()
 
 
-def dyn_run(state, near_row, near_col, point):
+def dyn_run(state, near_row, point):
     rows, cols, nodes, width = state.shape
     vmem = pl.BlockSpec(memory_space=pltpu.VMEM)
     smem = pl.BlockSpec(memory_space=pltpu.SMEM)
-    halo = pltpu.VMEM((rows + 2, cols + 2, nodes, width), jnp.float32)
+    halo = pltpu.VMEM((rows + 2, cols * len(RIM) + 2 * SIDE, width), jnp.float32)
     return pl.pallas_call(
         functools.partial(dyn_kernel, lax.axis_size("face"), lax.axis_size("col")),
         out_shape=jax.ShapeDtypeStruct(state.shape, jnp.float32),
-        in_specs=[smem, smem, smem, vmem],
+        in_specs=[smem, smem, vmem],
         out_specs=vmem,
         scratch_shapes=[
             halo,
             halo,
             pltpu.VMEM(state.shape, jnp.float32),
-            pltpu.SemaphoreType.DMA((DSTEPS, len(DIRECTIONS))),
-            pltpu.SemaphoreType.DMA((DSTEPS, len(DIRECTIONS))),
+            pltpu.VMEM(state.shape, jnp.float32),
+            pltpu.SemaphoreType.DMA((DSTEPS, 8)),
+            pltpu.SemaphoreType.DMA((DSTEPS, 8)),
         ],
         compiler_params=pltpu.CompilerParams(
             collective_id=0, has_side_effects=True, vmem_limit_bytes=32 * 2**20
         ),
-    )(near_row, near_col, point, state)
+    )(near_row, point, state)
 
 
 def crm_kernel(force_ref, active_ref, state_hbm, out_hbm, tend_ref, held, first, final, begin, in_sem, out_sem):
@@ -267,7 +294,7 @@
             pltpu.SemaphoreType.DMA((4,)),
             pltpu.SemaphoreType.DMA((4,)),
         ],
-        compiler_params=pltpu.CompilerParams(vmem_limit_bytes=36 * 2**20),
+        compiler_params=pltpu.CompilerParams(vmem_limit_bytes=60 * 2**20),
     )(forcing, active.reshape(1, cols), state)
 
 
@@ -292,8 +319,7 @@
     state = dyn_run(
         dyn_state,
         jnp.broadcast_to((local_row + drow + 1)[..., None], shape).reshape(-1),
-        jnp.broadcast_to((local_col + dcol + 1)[..., None], shape).reshape(-1),
-        pick.reshape(-1),
+        ((local_col + dcol)[..., None] * len(RIM) + SIDE + pick).reshape(-1),
     )
     columns = jnp.einsum("qn,rcnw->rcqw", quarter, state, precision=exact).reshape(-1, width)
     per_dev = columns.shape[0]

time: 115 us -> 104 us (0.904)
  Pallas kernels: 73.2 us -> 61.9 us
  local copies, waits for them, and re-layouts: 8.92 us -> 6.4 us
  blocking collectives: 12.9 us -> 14.7 us
  matrix products: 4.8 us -> 6.39 us
    pallas_call x1, Pallas kernels: 57.5 us -> 43.3 us  [dyn_run(): pl.pallas_call(functools.partial(dyn_kernel, lax.axis_size('face'), lax.a...]
    pallas_call x1, Pallas kernels: 15.7 us -> 18.7 us  [crm_run(): pl.pallas_call(crm_kernel, out_shape=(jax.ShapeDtypeStruct(state.shape, s...]
    unnamed x12 -> x8, local copies, waits for them, and re-layouts: 6 us -> 3.49 us
    all_to_all x1, blocking collectives: 12.9 us -> 14.7 us  [per_device(): lax.all_to_all(outgoing.reshape(ndev, count, depth + 1), ('face', 'col'),...]
where the time goes in v3:
time: 104 us
  Pallas kernels  61.9 us (60%)
  blocking collectives  14.7 us (14%)
  waiting for transfers between devices  8.84 us (8%)
  local copies, waits for them, and re-layouts  6.4 us (6%)
  matrix products  6.39 us (6%)
  other arithmetic  2.37 us (2%)
  starting transfers between devices  2.32 us (2%)
    pallas_call x1, Pallas kernels, dyn_run(): pl.pallas_call(functools.partial(dyn_kernel, lax.axis_size('face'), lax.a...  43.3 us
    pallas_call x1, Pallas kernels, crm_run(): pl.pallas_call(crm_kernel, out_shape=(jax.ShapeDtypeStruct(state.shape, s...  18.7 us
    all_to_all x1, blocking collectives, per_device(): lax.all_to_all(outgoing.reshape(ndev, count, depth + 1), ('face', 'col'),...  14.7 us
    all_to_all x1, waiting for transfers between devices, per_device(): lax.all_to_all(tend_rows.reshape(ndev, count, depth), ('face', 'col'), sp...  8.84 us
    unnamed x8, local copies, waits for them, and re-layouts  3.49 us
    all_to_all x1, starting transfers between devices, per_device(): lax.all_to_all(tend_rows.reshape(ndev, count, depth), ('face', 'col'), sp...  2.32 us
  transfers between devices with their start and end apart: 1, of which 1 were waited for; matrix products, arithmetic and copies ran while one was open for 0% of the time, Pallas kernels for 0%

profile of v3, /device:TPU:1, one launch (start us, length us, event | category | flops | bytes accessed | tf_op | source)
XLA Modules:
  0.0 103.8 jit_solution(8408046759621140047)
XLA Ops:
  0.7 0.7 fusion.30
  1.4 0.8 select_select_fusion
  2.2 0.1 copy.58
  2.4 0.1 reshape.106.row_ref
  2.5 0.1 copy.59
  2.7 0.1 add.117
  3.0 0.1 copy.62
  3.2 0.2 multiply_add_fusion
  3.3 0.1 add.122
  3.4 0.8 copy.63
  4.2 0.1 lt.48
  4.3 0.2 convert_reduce_fusion
  4.5 0.1 select_reduce_fusion
  4.7 0.3 convert_element_type.28
  4.9 1.4 %copy-done = f32[4,8,16,720]{3,2,1,0:T(8,128)S(1)} copy-done((f32[4,8,16,720]{3,2,1,0:T(8,128)S(1)}, f32[4,8,16,720]{3,2,1,0:T(8,128)}, u32[]{:S(2)}) %copy-start) | copy-done | bytes 1474584
  6.3 43.3 %shard_map.94 = f32[4,8,16,720]{3,2,1,0:T(8,128)S(1)} custom-call(s32[512]{0:T(512)S(1)} %reshape.106.row_ref, s32[512]{0:T(512)S(1)} %subtract_add_fusion.point_ref, f32[4,8,16,720]{3,2,1,0:T(8,128)S(1)} %copy-done), custom_call_target="tpu_custom_call" | custom-call | tf_op jit(solution)/shard_map/pallas_call | solution.py:179
  49.6 0.9 convolution_bitcast_fusion
  50.6 0.1 reshape.107
  50.7 0.1 copy-done.1
  50.9 2.0 %fusion.32 = f32[128,320]{0,1:T(8,128)S(1)} fusion(f32[128,720]{1,0:T(8,128)S(1)} %reshape.107, f32[720,320]{1,0:T(8,128)S(1)} %copy-done.1), kind=kOutput, calls=%fused_computation.77 | convolution fusion | flops 353894400 | bytes 1454080 | tf_op jit(solution)/shard_map/dot_general | solution.py:335
  52.9 0.3 fusion.6
  53.2 0.1 pad_maximum_fusion
  53.3 14.7 %all_to_all.10 = f32[32,4,321]{2,1,0:T(4,128)S(1)} all-to-all(f32[32,4,321]{2,1,0:T(4,128)S(1)} %pad_maximum_fusion), channel_id=1, replica_groups=mesh['face'=4,'col'=8] {'face','col'}, dimensions={0} | all-to-all | bytes 328704 | tf_op jit(solution)/shard_map/all_to_all | solution.py:337
  68.0 0.2 fusion.5
  68.2 1.0 %fusion = f32[320,128]{1,0:T(8,128)} fusion(f32[128,321]{1,0:T(8,128)S(1)} %reshape.108, s32[128]{0:T(128)S(1)} %fusion.5), kind=kOutput, calls=%fused_computation.1 | convolution fusion | flops 62930944 | bytes 328704 | tf_op jit(solution)/shard_map/sw,sc->wc/dot_general | solution.py:346
  69.4 18.7 %shard_map.95 = (bf16[10,32,64,128]{3,2,1,0:T(8,128)(2,1)}, f32[10,32,128]{2,1,0:T(8,128)}) custom-call(f32[10,32,128]{2,1,0:T(8,128)} %bitcast.24, s32[1,128]{1,0:T(1,128)} %bitcast.26, bf16[10,32,64,128]{3,2,1,0:T(8,128)(2,1)} %state_hbm.1), custom_call_target="tpu_custom_call" | custom-call | tf_op jit(solution)/shard_map/pallas_call | solution.py:281
  88.1 1.2 %fusion.9 = f32[32,4,320]{2,0,1:T(8,128)S(1)} fusion(f32[320,128,1]{1,0,2:T(8,128)} %bitcast.25, s32[32,4]{0,1:T(4,128)S(1)} %copy.67), kind=kOutput, calls=%fused_computation.22 | convolution fusion | flops 62930944 | bytes 328192 | tf_op jit(solution)/shard_map/sc,wc->sw/dot_general | solution.py:348
  89.3 0.8 copy.68
  90.1 2.3 %all-to-all-start.1 = ((f32[32,4,320]{2,1,0:T(4,128)}), f32[32,4,320]{2,1,0:T(4,128)S(1)}, u32[]{:S(2)}, u32[]{:S(2)}) async-start(f32[32,4,320]{2,1,0:T(4,128)} %copy.68), calls=%async_computation.1 | async-start | bytes 393216 | tf_op jit(solution)/shard_map/all_to_all | solution.py:349
  92.8 8.8 %all-to-all-done.1 = f32[32,4,320]{2,1,0:T(4,128)S(1)} async-done(((f32[32,4,320]{2,1,0:T(4,128)}), f32[32,4,320]{2,1,0:T(4,128)S(1)}, u32[]{:S(2)}, u32[]{:S(2)}) %all-to-all-start.1) | async-done | bytes 163872 | tf_op jit(solution)/shard_map/all_to_all | solution.py:349
  101.7 1.0 fusion.2
  102.6 1.1 %copy.80 = f32[4,8,16,720]{3,2,1,0:T(8,128)} copy(f32[4,8,16,720]{3,2,1,0:T(8,128)S(1)} %shard_map.94) | data formatting | bytes 2949120
  (22 shorter events, 1.1 us)
Async XLA Ops:
  4.9 1.4 %copy-start = (f32[4,8,16,720]{3,2,1,0:T(8,128)S(1)}, f32[4,8,16,720]{3,2,1,0:T(8,128)}, u32[]{:S(2)}) copy-start(f32[4,8,16,720]{3,2,1,0:T(8,128)} %state_ref.1) | copy-start | bytes 4423684
  6.3 43.3 %copy-start.2 = (f32[4,16,1,1]{1,0,3,2:T(4,128)S(1)}, f32[4,16,1,1]{1,0,3,2:T(4,128)}, u32[]{:S(2)}) copy-start(f32[4,16,1,1]{1,0,3,2:T(4,128)} %constant.133) | copy-start | bytes 772
  49.6 1.2 %copy-start.1 = (f32[720,320]{1,0:T(8,128)S(1)}, f32[720,320]{1,0:T(8,128)}, u32[]{:S(2)}) copy-start(f32[720,320]{1,0:T(8,128)} %constant.132.clone) | copy-start | bytes 2764804
  90.1 11.5 %all-to-all-start.1 = ((f32[32,4,320]{2,1,0:T(4,128)}), f32[32,4,320]{2,1,0:T(4,128)S(1)}, u32[]{:S(2)}, u32[]{:S(2)}) async-start(f32[32,4,320]{2,1,0:T(4,128)} %copy.68), calls=%async_computation.1 | async-start | bytes 393216 | tf_op jit(solution)/shard_map/all_to_all | solution.py:349

commit v4 on v3

--- a/solution.py
+++ b/solution.py
@@ -197,7 +197,7 @@
 
 def crm_kernel(force_ref, active_ref, state_hbm, out_hbm, tend_ref, held, first, final, begin, in_sem, out_sem):
     nfld, clev, cx, cols = held.shape
-    part = clev // 4
+    part = clev // 8
 
     def fetch(i):
         return pltpu.make_async_copy(
@@ -209,7 +209,7 @@
             final.at[:, pl.ds(i * part, part)], out_hbm.at[:, pl.ds(i * part, part)], out_sem.at[i]
         )
 
-    for i in range(4):
+    for i in range(8):
         fetch(i).start()
     live = jnp.broadcast_to(active_ref[...] == 1, (cx, cols))
 
@@ -257,8 +257,8 @@
     fetch(0).wait()
     fetch(1).wait()
     advance(held, 0, store_first)
-    for i in range(4):
-        if 1 <= i < 3:
+    for i in range(8):
+        if 1 <= i < 7:
             fetch(i + 1).wait()
 
         @pl.loop(max(1, i * part), (i + 1) * part)
@@ -269,8 +269,8 @@
         if i >= 1:
             emit(i - 1).start()
     advance(first, clev - 1, store_final)
-    emit(3).start()
-    for i in range(4):
+    emit(7).start()
+    for i in range(8):
         emit(i).wait()
 
 
@@ -291,8 +291,8 @@
             pltpu.VMEM(state.shape, jnp.float32),
             pltpu.VMEM(state.shape, state.dtype),
             pltpu.VMEM((nfld, clev, cols), jnp.float32),
-            pltpu.SemaphoreType.DMA((4,)),
-            pltpu.SemaphoreType.DMA((4,)),
+            pltpu.SemaphoreType.DMA((8,)),
+            pltpu.SemaphoreType.DMA((8,)),
         ],
         compiler_params=pltpu.CompilerParams(vmem_limit_bytes=60 * 2**20),
     )(forcing, active.reshape(1, cols), state)

time: 104 us -> 103 us (level)
  no operation moved by 1% of the time
where the time goes in v4:
time: 103 us
  Pallas kernels  61.1 us (59%)
  blocking collectives  14.7 us (14%)
  waiting for transfers between devices  8.84 us (9%)
  local copies, waits for them, and re-layouts  6.4 us (6%)
  matrix products  6.39 us (6%)
  other arithmetic  2.37 us (2%)
  starting transfers between devices  2.32 us (2%)
    pallas_call x1, Pallas kernels, dyn_run(): pl.pallas_call(functools.partial(dyn_kernel, lax.axis_size('face'), lax.a...  43.3 us
    pallas_call x1, Pallas kernels, crm_run(): pl.pallas_call(crm_kernel, out_shape=(jax.ShapeDtypeStruct(state.shape, s...  17.9 us
    all_to_all x1, blocking collectives, per_device(): lax.all_to_all(outgoing.reshape(ndev, count, depth + 1), ('face', 'col'),...  14.7 us
    all_to_all x1, waiting for transfers between devices, per_device(): lax.all_to_all(tend_rows.reshape(ndev, count, depth), ('face', 'col'), sp...  8.84 us
    unnamed x8, local copies, waits for them, and re-layouts  3.49 us
    all_to_all x1, starting transfers between devices, per_device(): lax.all_to_all(tend_rows.reshape(ndev, count, depth), ('face', 'col'), sp...  2.32 us
  transfers between devices with their start and end apart: 1, of which 1 were waited for; matrix products, arithmetic and copies ran while one was open for 0% of the time, Pallas kernels for 0%

profile of v4, /device:TPU:1, one launch (start us, length us, event | category | flops | bytes accessed | tf_op | source)
XLA Modules:
  0.0 103.0 jit_solution(2683876902213275531)
XLA Ops:
  0.7 0.7 fusion.30
  1.4 0.8 select_select_fusion
  2.2 0.1 copy.58
  2.4 0.1 reshape.106.row_ref
  2.5 0.1 copy.59
  2.7 0.1 add.117
  3.0 0.1 copy.62
  3.2 0.2 multiply_add_fusion
  3.3 0.1 add.122
  3.4 0.8 copy.63
  4.2 0.1 lt.48
  4.3 0.2 convert_reduce_fusion
  4.5 0.1 select_reduce_fusion
  4.7 0.3 convert_element_type.28
  4.9 1.4 %copy-done = f32[4,8,16,720]{3,2,1,0:T(8,128)S(1)} copy-done((f32[4,8,16,720]{3,2,1,0:T(8,128)S(1)}, f32[4,8,16,720]{3,2,1,0:T(8,128)}, u32[]{:S(2)}) %copy-start) | copy-done | bytes 1474584
  6.3 43.3 %shard_map.94 = f32[4,8,16,720]{3,2,1,0:T(8,128)S(1)} custom-call(s32[512]{0:T(512)S(1)} %reshape.106.row_ref, s32[512]{0:T(512)S(1)} %subtract_add_fusion.point_ref, f32[4,8,16,720]{3,2,1,0:T(8,128)S(1)} %copy-done), custom_call_target="tpu_custom_call" | custom-call | tf_op jit(solution)/shard_map/pallas_call | solution.py:179
  49.6 0.9 convolution_bitcast_fusion
  50.6 0.1 reshape.107
  50.7 0.1 copy-done.1
  50.9 2.0 %fusion.32 = f32[128,320]{0,1:T(8,128)S(1)} fusion(f32[128,720]{1,0:T(8,128)S(1)} %reshape.107, f32[720,320]{1,0:T(8,128)S(1)} %copy-done.1), kind=kOutput, calls=%fused_computation.77 | convolution fusion | flops 353894400 | bytes 1454080 | tf_op jit(solution)/shard_map/dot_general | solution.py:335
  52.9 0.3 fusion.6
  53.2 0.1 pad_maximum_fusion
  53.3 14.7 %all_to_all.10 = f32[32,4,321]{2,1,0:T(4,128)S(1)} all-to-all(f32[32,4,321]{2,1,0:T(4,128)S(1)} %pad_maximum_fusion), channel_id=1, replica_groups=mesh['face'=4,'col'=8] {'face','col'}, dimensions={0} | all-to-all | bytes 328704 | tf_op jit(solution)/shard_map/all_to_all | solution.py:337
  68.0 0.2 fusion.5
  68.2 1.0 %fusion = f32[320,128]{1,0:T(8,128)} fusion(f32[128,321]{1,0:T(8,128)S(1)} %reshape.108, s32[128]{0:T(128)S(1)} %fusion.5), kind=kOutput, calls=%fused_computation.1 | convolution fusion | flops 62930944 | bytes 328704 | tf_op jit(solution)/shard_map/sw,sc->wc/dot_general | solution.py:346
  69.4 17.9 %shard_map.95 = (bf16[10,32,64,128]{3,2,1,0:T(8,128)(2,1)}, f32[10,32,128]{2,1,0:T(8,128)}) custom-call(f32[10,32,128]{2,1,0:T(8,128)} %bitcast.24, s32[1,128]{1,0:T(1,128)} %bitcast.26, bf16[10,32,64,128]{3,2,1,0:T(8,128)(2,1)} %state_hbm.1), custom_call_target="tpu_custom_call" | custom-call | tf_op jit(solution)/shard_map/pallas_call | solution.py:281
  87.3 1.2 %fusion.9 = f32[32,4,320]{2,0,1:T(8,128)S(1)} fusion(f32[320,128,1]{1,0,2:T(8,128)} %bitcast.25, s32[32,4]{0,1:T(4,128)S(1)} %copy.67), kind=kOutput, calls=%fused_computation.22 | convolution fusion | flops 62930944 | bytes 328192 | tf_op jit(solution)/shard_map/sc,wc->sw/dot_general | solution.py:348
  88.5 0.8 copy.68
  89.3 2.3 %all-to-all-start.1 = ((f32[32,4,320]{2,1,0:T(4,128)}), f32[32,4,320]{2,1,0:T(4,128)S(1)}, u32[]{:S(2)}, u32[]{:S(2)}) async-start(f32[32,4,320]{2,1,0:T(4,128)} %copy.68), calls=%async_computation.1 | async-start | bytes 393216 | tf_op jit(solution)/shard_map/all_to_all | solution.py:349
  92.0 8.8 %all-to-all-done.1 = f32[32,4,320]{2,1,0:T(4,128)S(1)} async-done(((f32[32,4,320]{2,1,0:T(4,128)}), f32[32,4,320]{2,1,0:T(4,128)S(1)}, u32[]{:S(2)}, u32[]{:S(2)}) %all-to-all-start.1) | async-done | bytes 163872 | tf_op jit(solution)/shard_map/all_to_all | solution.py:349
  100.9 1.0 fusion.2
  101.8 1.1 %copy.80 = f32[4,8,16,720]{3,2,1,0:T(8,128)} copy(f32[4,8,16,720]{3,2,1,0:T(8,128)S(1)} %shard_map.94) | data formatting | bytes 2949120
  (22 shorter events, 1.1 us)
Async XLA Ops:
  4.9 1.4 %copy-start = (f32[4,8,16,720]{3,2,1,0:T(8,128)S(1)}, f32[4,8,16,720]{3,2,1,0:T(8,128)}, u32[]{:S(2)}) copy-start(f32[4,8,16,720]{3,2,1,0:T(8,128)} %state_ref.1) | copy-start | bytes 4423684
  6.3 43.3 %copy-start.2 = (f32[4,16,1,1]{1,0,3,2:T(4,128)S(1)}, f32[4,16,1,1]{1,0,3,2:T(4,128)}, u32[]{:S(2)}) copy-start(f32[4,16,1,1]{1,0,3,2:T(4,128)} %constant.133) | copy-start | bytes 772
  49.6 1.2 %copy-start.1 = (f32[720,320]{1,0:T(8,128)S(1)}, f32[720,320]{1,0:T(8,128)}, u32[]{:S(2)}) copy-start(f32[720,320]{1,0:T(8,128)} %constant.132.clone) | copy-start | bytes 2764804
  89.3 11.5 %all-to-all-start.1 = ((f32[32,4,320]{2,1,0:T(4,128)}), f32[32,4,320]{2,1,0:T(4,128)S(1)}, u32[]{:S(2)}, u32[]{:S(2)}) async-start(f32[32,4,320]{2,1,0:T(4,128)} %copy.68), calls=%async_computation.1 | async-start | bytes 393216 | tf_op jit(solution)/shard_map/all_to_all | solution.py:349
